TPU v7x, 128 devices: a whole 4x4x4 slice. The times are simulated.
128 devices in a mesh: dp: 8 (over x, core), shard: 2 (over z_lo), ctx: 8 (over z_hi, y).
Axes of the slice: x: 4, y: 4, z: 4 (z_hi: 2, z_lo: 2; z = z_hi * 2 + z_lo), core: 2. Of those that a mesh axis runs over, the one named last changes fastest.
Arguments:
- inputs: bfloat16 [16384, 4096], P(('dp', 'shard', 'ctx')), may hold values from -24 to 24
- queries: bfloat16 [16384, 4096], P(('dp', 'shard', 'ctx')), may hold values from -272 to 272
- out_grad: bfloat16 [16384, 4096], P(('dp', 'shard', 'ctx')), may hold values from -6 to 6
- span_ids: int32 [8, 16, 2], P('dp'), may hold values from 0 to 31, as said below
- norm_gain: bfloat16 [4096], P(('shard', 'ctx')), may hold values from 0.5 to 1.5
- key_weight: bfloat16 [4096, 512], P(('shard', 'ctx')), may hold values from -0.09375 to 0.09375
- value_weight: bfloat16 [4096, 512], P(('shard', 'ctx')), may hold values from -0.09375 to 0.09375
Outputs:
- attention_out: bfloat16 [16384, 4096], P(('dp', 'shard', 'ctx'))
- query_grad: bfloat16 [16384, 4096], P(('dp', 'shard', 'ctx'))
- input_grad: bfloat16 [16384, 4096], P(('dp', 'shard', 'ctx'))
- key_weight_grad: float32 [4096, 512], P(('shard', 'ctx'))
- value_weight_grad: float32 [4096, 512], P(('shard', 'ctx'))
- gain_grad: float32 [4096], P(('shard', 'ctx'))
Inputs may be any that keep to these rules, and one draw needn't show every extreme that they name: `span_ids`: in each replica the 16 rows together hold every span number once; a row holds some c and 31 - c, in either order.
All inputs are finite; a program needn't handle non-finite values.
Results may differ from a plain program's by a relative error of at most 0.012.
The roundings to bfloat16 on the way count: a program that leaves them out, or rounds other values in their place, can miss the bound.
Values may be sent and summed in bfloat16 or wider, within the bound.
A program may use at most 128 MiB of HBM per device.

v0:
```python
import math

import jax
import jax.numpy as jnp
from jax import lax
from jax.sharding import PartitionSpec as P

HEAD_DIM = 128


EPSILON = 1e-05
ROPE_BASE = 500000.0
NEG_FILL = -1e30


def rope_tables(positions, head_size):
    half = head_size // 2
    frequency = jnp.exp(
        -math.log(ROPE_BASE) * (2.0 * jnp.arange(half, dtype=jnp.float32) / head_size)
    )
    angles = positions.astype(jnp.float32)[:, None] * frequency[None, :]
    return (jnp.cos(angles)[:, None, :], jnp.sin(angles)[:, None, :])


def rotate(vectors, cosine, sine, direction):
    half = vectors.shape[-1] // 2
    first = vectors[..., :half]
    second = vectors[..., half:]
    return jnp.concatenate(
        [first * cosine - direction * second * sine, second * cosine + direction * first * sine],
        axis=-1,
    )


def token_positions(table, row_index, half_rows):
    owners = jnp.arange(table.shape[0], dtype=jnp.int32)
    match = (row_index // half_rows)[:, None] == owners[None, :]
    span_number = jnp.sum(jnp.where(match, table[None, :], 0), axis=1)
    return span_number * half_rows + row_index % half_rows


def over_blocks(step, state, piece):
    count = piece.shape[0]
    width = 512
    blocks = piece.reshape(count // width, width, piece.shape[1])
    offsets = width * jnp.arange(count // width, dtype=jnp.int32)

    def advance(inner, operand):
        return (step(inner, operand[0], operand[1]), None)

    state, unused = lax.scan(advance, state, (blocks, offsets))
    return state


def local(inputs, queries, out_grad, span_ids, norm_gain, key_weight, value_weight):
    ranks = lax.axis_size(("shard", "ctx"))
    rank = lax.axis_index(("shard", "ctx"))
    tokens = inputs.shape[0]
    half_rows = tokens // 2
    kv_width = key_weight.shape[1]
    kv_heads = kv_width // HEAD_DIM
    heads = queries.shape[1] // HEAD_DIM
    group = heads // kv_heads
    scale = HEAD_DIM ** (-0.5)
    table = span_ids.reshape(-1)
    own_rows = rank * tokens + jnp.arange(tokens, dtype=jnp.int32)
    own_positions = token_positions(table, own_rows, half_rows)
    cosine, sine = rope_tables(own_positions, HEAD_DIM)
    gain_all, key_all, value_all = (
        lax.all_gather(norm_gain, ("shard", "ctx"), axis=0, tiled=True),
        lax.all_gather(key_weight, ("shard", "ctx"), axis=0, tiled=True),
        lax.all_gather(value_weight, ("shard", "ctx"), axis=0, tiled=True),
    )
    input_f = inputs.astype(jnp.float32)
    inverse_rms = lax.rsqrt(jnp.mean(input_f * input_f, axis=-1, keepdims=True) + EPSILON)
    unit_rows = input_f * inverse_rms
    gain_f = gain_all.astype(jnp.float32)
    normed = (unit_rows * gain_f).astype(jnp.bfloat16)
    key_raw = jnp.dot(normed, key_all, preferred_element_type=jnp.float32)
    value_raw = jnp.dot(normed, value_all, preferred_element_type=jnp.float32)
    keys = (
        rotate(key_raw.reshape(tokens, kv_heads, HEAD_DIM), cosine, sine, 1.0)
        .astype(jnp.bfloat16)
        .reshape(tokens, kv_width)
    )
    values = value_raw.astype(jnp.bfloat16)
    kv_local = jnp.concatenate([keys, values], axis=1)
    grouped_q = queries.reshape(tokens, kv_heads, group, HEAD_DIM)
    grouped_g = out_grad.reshape(tokens, kv_heads, group, HEAD_DIM)

    def score_block(piece, start):
        count = piece.shape[0]
        key_rows = start + jnp.arange(count, dtype=jnp.int32)
        key_positions = token_positions(table, key_rows, half_rows)
        visible = key_positions[None, :] <= own_positions[:, None]
        key_part = piece[:, :kv_width].reshape(count, kv_heads, HEAD_DIM)
        value_part = piece[:, kv_width:].reshape(count, kv_heads, HEAD_DIM)
        scores = (
            jnp.einsum("tkgd,nkd->kgtn", grouped_q, key_part, preferred_element_type=jnp.float32)
            * scale
        )
        return (scores, visible, key_part, value_part)

    def forward_step(state, piece, start):
        running_max, running_sum, weighted = state
        scores, visible, key_part, value_part = score_block(piece, start)
        block_max = jnp.max(jnp.where(visible, scores, NEG_FILL), axis=-1)
        new_max = jnp.maximum(running_max, block_max)
        decay = jnp.exp(running_max - new_max)
        weights = jnp.where(visible, jnp.exp(scores - new_max[..., None]), 0.0)
        running_sum = running_sum * decay + jnp.sum(weights, axis=-1)
        weighted = weighted * decay[..., None] + jnp.einsum(
            "kgtn,nkd->kgtd",
            weights.astype(jnp.bfloat16),
            value_part,
            preferred_element_type=jnp.float32,
        )
        return (new_max, running_sum, weighted)

    forward_start = (
        jnp.full((kv_heads, group, tokens), NEG_FILL, jnp.float32),
        jnp.zeros((kv_heads, group, tokens), jnp.float32),
        jnp.zeros((kv_heads, group, tokens, HEAD_DIM), jnp.float32),
    )
    kv_whole = lax.all_gather(kv_local, ("shard", "ctx"), axis=0, tiled=True)
    running_max, running_sum, weighted = over_blocks(forward_step, forward_start, kv_whole)
    attended = (
        (weighted / running_sum[..., None])
        .transpose(2, 0, 1, 3)
        .reshape(tokens, heads * HEAD_DIM)
        .astype(jnp.bfloat16)
    )
    attended_f = (
        lax.optimization_barrier(attended)
        .astype(jnp.float32)
        .reshape(tokens, kv_heads, group, HEAD_DIM)
    )
    log_total = running_max + jnp.log(running_sum)
    grad_f = grouped_g.astype(jnp.float32)
    row_dots = jnp.sum(grad_f * attended_f, axis=-1).transpose(1, 2, 0)

    def backward_step(state, piece, start):
        query_acc, kv_acc = state
        scores, visible, key_part, value_part = score_block(piece, start)
        probs = jnp.where(visible, jnp.exp(scores - log_total[..., None]), 0.0)
        value_dots = jnp.einsum(
            "tkgd,nkd->kgtn", grouped_g, value_part, preferred_element_type=jnp.float32
        )
        score_grad = (probs * (value_dots - row_dots[..., None]) * scale).astype(jnp.bfloat16)
        query_acc = query_acc + jnp.einsum(
            "kgtn,nkd->kgtd", score_grad, key_part, preferred_element_type=jnp.float32
        )
        key_grad = jnp.einsum(
            "kgtn,tkgd->nkd", score_grad, grouped_q, preferred_element_type=jnp.float32
        )
        value_grad = jnp.einsum(
            "kgtn,tkgd->nkd",
            probs.astype(jnp.bfloat16),
            grouped_g,
            preferred_element_type=jnp.float32,
        )
        count = piece.shape[0]
        update = jnp.concatenate(
            [key_grad.reshape(count, kv_width), value_grad.reshape(count, kv_width)], axis=1
        )
        current = lax.dynamic_slice_in_dim(kv_acc, start, count, 0)
        kv_acc = lax.dynamic_update_slice_in_dim(kv_acc, current + update, start, 0)
        return (query_acc, kv_acc)

    backward_start = (
        jnp.zeros((kv_heads, group, tokens, HEAD_DIM), jnp.float32),
        jnp.zeros((tokens * ranks, 2 * kv_width), jnp.float32),
    )
    query_acc, kv_acc = over_blocks(backward_step, backward_start, kv_whole)
    query_grad = (
        query_acc.transpose(2, 0, 1, 3).reshape(tokens, heads * HEAD_DIM).astype(jnp.bfloat16)
    )
    kv_grad = lax.psum_scatter(kv_acc, ("shard", "ctx"), scatter_dimension=0, tiled=True)
    key_grad = (
        rotate(kv_grad[:, :kv_width].reshape(tokens, kv_heads, HEAD_DIM), cosine, sine, -1.0)
        .reshape(tokens, kv_width)
        .astype(jnp.bfloat16)
    )
    value_grad = kv_grad[:, kv_width:].astype(jnp.bfloat16)
    contract_cols = (((1,), (1,)), ((), ()))
    normed_grad = lax.dot_general(
        key_grad, key_all, contract_cols, preferred_element_type=jnp.float32
    ) + lax.dot_general(value_grad, value_all, contract_cols, preferred_element_type=jnp.float32)
    gain_term = jnp.sum(unit_rows * normed_grad, axis=0)
    unit_grad = normed_grad * gain_f
    input_grad = (
        inverse_rms
        * (unit_grad - unit_rows * jnp.mean(unit_grad * unit_rows, axis=-1, keepdims=True))
    ).astype(jnp.bfloat16)
    contract_rows = (((0,), (0,)), ((), ()))
    key_term = lax.dot_general(normed, key_grad, contract_rows, preferred_element_type=jnp.float32)
    value_term = lax.dot_general(
        normed, value_grad, contract_rows, preferred_element_type=jnp.float32
    )
    key_share, value_share, gain_share = (
        lax.psum_scatter(key_term, ("shard", "ctx"), scatter_dimension=0, tiled=True),
        lax.psum_scatter(value_term, ("shard", "ctx"), scatter_dimension=0, tiled=True),
        lax.psum_scatter(gain_term, ("shard", "ctx"), scatter_dimension=0, tiled=True),
    )
    key_sum, value_sum, gain_sum = lax.psum((key_share, value_share, gain_share), "dp")
    return (attended, query_grad, input_grad, key_sum, value_sum, gain_sum)


def solution(mesh):
    placed = (
        P(("dp", "shard", "ctx"), None),
        P(("dp", "shard", "ctx"), None),
        P(("dp", "shard", "ctx"), None),
        P("dp", None, None),
        P(("shard", "ctx")),
        P(("shard", "ctx"), None),
        P(("shard", "ctx"), None),
    )
    return jax.shard_map(
        local,
        mesh=mesh,
        in_specs=placed,
        out_specs=(
            P(("dp", "shard", "ctx"), None),
            P(("dp", "shard", "ctx"), None),
            P(("dp", "shard", "ctx"), None),
            P(("shard", "ctx"), None),
            P(("shard", "ctx"), None),
            P(("shard", "ctx")),
        ),
        check_vma=False,
    )
```

profile of v0, /device:TPU:1, one launch (start us, length us, event | category | flops | bytes accessed | tf_op | source)
XLA Modules:
  0.0 842.7 jit_solution(3568716274583993068)
XLA Ops:
  10.2 35.5 %all-gather = bf16[16,1,256]{2,1,0:T(2,128)(2,1)S(1)} all-gather(bf16[1,1,256]{2,1,0:T(2,128)(2,1)S(1)} %reshape.268), channel_id=1, replica_groups=mesh['dp'=8,'shard'=2,'ctx'=8] {'shard','ctx'}, dimensions={0}, use_global_device_ids=true | all-gather | bytes 8704 | tf_op jit(solution)/shard_map/all_gather | solution.py:70
  45.9 1.5 fusion.46
  48.4 37.2 %all-gather.5.cloned.1.call-done = bf16[4096,512]{1,0:T(8,128)(2,1)} async-done(((bf16[256,512]{1,0:T(8,128)(2,1)}), bf16[4096,512]{1,0:T(8,128)(2,1)}) %all-gather.5.cloned.1.call-update) | async-done | bytes 4194320 | tf_op jit(solution)/shard_map/all_gather | solution.py:71
  85.6 3.3 fusion.59
  89.5 80.3 %all-gather.7.cloned.1.call-done = bf16[4096,512]{1,0:T(8,128)(2,1)} async-done(((bf16[256,512]{1,0:T(8,128)(2,1)}), bf16[4096,512]{1,0:T(8,128)(2,1)}) %all-gather.7.cloned.1.call-update) | async-done | bytes 4194320 | tf_op jit(solution)/shard_map/all_gather | solution.py:72
  169.8 3.0 convolution_convert_fusion
  176.6 79.8 %all-gather.9.cloned.1.call-done = bf16[2048,1024]{1,0:T(8,128)(2,1)} async-done(((bf16[128,1024]{1,0:T(8,128)(2,1)}), bf16[2048,1024]{1,0:T(8,128)(2,1)}) %all-gather.9.cloned.1.call-update) | async-done | bytes 4194320 | tf_op jit(solution)/shard_map/all_gather | solution.py:125
  256.4 6.3 copy.92
  262.7 45.1 %while.34 = (s32[]{:T(128)}, f32[4,8,128]{2,1,0:T(8,128)S(1)}, f32[4,8,128]{2,1,0:T(8,128)S(1)}, f32[4,8,128,128]{3,2,1,0:T(8,128)}, s32[4]{0:T(128)S(1)}, /*ind...) while((s32[]{:T(128)}, f32[4,8,128]{2,1,0:T(8,128)S(1)}, ...), condition=%wide.wide.region_6.7_spmd.clone, body=%wide.wide.region_2.6_spmd.clone.sunk | while | flops 1098533376 | bytes 52966232 | solution.py:51
  266.2 1.5 fusion.142
  267.7 1.8 fusion.143
  269.5 3.1 fusion.145
  277.4 1.5 fusion.142
  278.9 1.8 fusion.143
  280.7 3.1 fusion.145
  288.7 1.5 fusion.142
  290.2 1.8 fusion.143
  292.0 3.1 fusion.145
  300.0 1.5 fusion.142
  301.5 1.8 fusion.143
  303.3 3.1 fusion.145
  307.7 1.9 fusion.47
  311.8 1.5 copy.115
  313.3 1.5 multiply_reduce_fusion
  314.8 4.3 broadcast_in_dim.126
  319.1 130.0 %while.35 = (s32[]{:T(128)}, f32[4,8,128,128]{3,2,1,0:T(8,128)}, f32[2048,1024]{0,1:T(8,128)}, s32[4]{0:T(128)S(1)}, s32[1,16,2]{2,1,0:T(8,128)}, /*index=5*/s32...) while((s32[]{:T(128)}, f32[4,8,128,128]{3,2,1,0:T(8,128)}, ...), condition=%wide.wide.region_10.11_spmd.clone, body=%wide.wide.region_8.10_spmd.clone.sunk | while | flops 2709649920 | bytes 64746332 | solution.py:51
  325.9 3.0 fusion.160
  328.9 4.4 fusion.159
  333.3 1.5 fusion.161
  334.8 3.0 select_add_fusion.3
  337.8 2.4 maximum_add_fusion.3
  340.2 10.5 %dynamic_update_slice.9 = f32[2048,1024]{0,1:T(8,128)} dynamic-update-slice(f32[2048,1024]{0,1:T(8,128)} %get-tuple-element.771, f32[512,1024]{0,1:T(8,128)S(1)} %maximum_add_fusion.3, s32[]{:T(128)S(6)} %select_n.194, s32[]{:T(128)} %constant.196.clone.1..sunk.1) | dynamic-update-slice | bytes 4194308 | tf_op jit(solution)/shard_map/while/body/eval_jaxpr/dynamic_update_slice | solution.py:167
  357.5 3.0 fusion.160
  360.5 4.4 fusion.159
  364.9 1.5 fusion.161
  366.4 4.6 select_add_fusion.3
  371.0 2.4 maximum_add_fusion.3
  373.4 10.5 %dynamic_update_slice.9 = f32[2048,1024]{0,1:T(8,128)} dynamic-update-slice(f32[2048,1024]{0,1:T(8,128)} %get-tuple-element.771, f32[512,1024]{0,1:T(8,128)S(1)} %maximum_add_fusion.3, s32[]{:T(128)S(6)} %select_n.194, s32[]{:T(128)} %constant.196.clone.1..sunk.1) | dynamic-update-slice | bytes 4194308 | tf_op jit(solution)/shard_map/while/body/eval_jaxpr/dynamic_update_slice | solution.py:167
  390.7 3.0 fusion.160
  393.7 4.4 fusion.159
  398.1 1.5 fusion.161
  399.6 4.6 select_add_fusion.3
  404.2 2.4 maximum_add_fusion.3
  406.6 10.5 %dynamic_update_slice.9 = f32[2048,1024]{0,1:T(8,128)} dynamic-update-slice(f32[2048,1024]{0,1:T(8,128)} %get-tuple-element.771, f32[512,1024]{0,1:T(8,128)S(1)} %maximum_add_fusion.3, s32[]{:T(128)S(6)} %select_n.194, s32[]{:T(128)} %constant.196.clone.1..sunk.1) | dynamic-update-slice | bytes 4194308 | tf_op jit(solution)/shard_map/while/body/eval_jaxpr/dynamic_update_slice | solution.py:167
  423.8 3.0 fusion.160
  426.8 4.4 fusion.159
  431.3 1.5 fusion.161
  432.8 4.6 select_add_fusion.3
  437.3 2.3 maximum_add_fusion.3
  439.6 9.5 %dynamic_update_slice.9 = f32[2048,1024]{0,1:T(8,128)} dynamic-update-slice(f32[2048,1024]{0,1:T(8,128)} %get-tuple-element.771, f32[512,1024]{0,1:T(8,128)S(1)} %maximum_add_fusion.3, s32[]{:T(128)S(6)} %select_n.194, s32[]{:T(128)} %constant.196.clone.1..sunk.1) | dynamic-update-slice | bytes 4194308 | tf_op jit(solution)/shard_map/while/body/eval_jaxpr/dynamic_update_slice | solution.py:167
  449.2 106.4 %reduce-scatter.4.cloned.1.call-done = f32[128,1024]{0,1:T(8,128)} async-done(((f32[2048,1024]{0,1:T(8,128)}), f32[128,1024]{0,1:T(8,128)}) %reduce-scatter.4.cloned.1.call-update) | async-done | bytes 524304 | tf_op jit(solution)/shard_map/reduce_scatter | solution.py:178
  555.7 5.5 fusion.54
  562.8 4.6 fusion.48
  569.4 1.9 convert_bitcast_fusion
  572.0 1.4 copy.143
  573.4 1.5 fusion.50
  574.9 1.8 fusion.45
  576.6 65.8 %all-reduce = f32[4096]{0:T(1024)S(1)} all-reduce(f32[4096]{0:T(1024)S(1)} %get-tuple-element.416), channel_id=5, replica_groups=mesh['dp'=8,'shard'=2,'ctx'=8] {'shard','ctx'}, use_global_device_ids=true, to_apply=%region_18.19.clone | all-reduce | flops 4096 | bytes 32768
  642.6 27.2 %psum.23 = f32[256]{0:T(256)} all-reduce(f32[256]{0:T(256)S(1)} %dynamic-slice.1), channel_id=1, replica_groups=mesh['dp'=8,'shard'=2,'ctx'=8] {'dp'}, use_global_device_ids=true, to_apply=%region_19.20 | all-reduce | flops 256 | bytes 2048 | tf_op jit(solution)/shard_map/psum | solution.py:205
  669.8 95.3 %reduce-scatter.6.cloned.1.call-done = f32[256,512]{1,0:T(8,128)} async-done(((f32[4096,512]{1,0:T(8,128)}), f32[256,512]{1,0:T(8,128)}) %reduce-scatter.6.cloned.1.call-update) | async-done | bytes 524304 | tf_op jit(solution)/shard_map/reduce_scatter | solution.py:201
  765.1 1.5 fusion.44
  766.6 65.5 %all-reduce.4.cloned.1.call-done = (f32[256,512]{1,0:T(8,128)}, f32[256,512]{1,0:T(8,128)}) async-done(((f32[256,512]{1,0:T(8,128)}, f32[256,512]{1,0:T(8,128)}), (f32[256,512]{1,0:T(8,128)}, f32[256,512]{1,0:T(8,128)})) %all-reduce.4.cloned.1.call-update) | async-done | bytes 1048592 | tf_op jit(solution)/shard_map/psum | solution.py:205
  832.1 1.9 copy.170
  834.0 1.9 copy.171
  (174 shorter events, 52.7 us)
Async XLA Ops:
  7.2 78.4 %all-gather.5.cloned.1.call-start = ((), (), s32[]{:S(2)}) async-start(), calls=%async_computation.3 | async-start | bytes 4456448 | tf_op jit(solution)/shard_map/all_gather | solution.py:71
  7.9 161.8 %all-gather.7.cloned.1.call-start = ((), (), s32[]{:S(2)}) async-start(), calls=%async_computation.4 | async-start | bytes 4456448 | tf_op jit(solution)/shard_map/all_gather | solution.py:72
  8.6 247.7 %all-gather.9.cloned.1.call-start = ((), (), s32[]{:S(2)}) async-start(), calls=%async_computation.5 | async-start | bytes 4456448 | tf_op jit(solution)/shard_map/all_gather | solution.py:125
  10.1 163.7 %copy-start.14 = (s32[1,16,2]{2,1,0:T(8,128)}, s32[1,16,2]{2,1,0:T(8,128)S(1)}, u32[]{:S(2)}) copy-start(s32[1,16,2]{2,1,0:T(8,128)S(1)} %copy.91) | copy-start | bytes 388
  45.7 124.0 %copy-start.9 = (f32[16,1,256]{2,1,0:T(1,128)}, f32[16,1,256]{2,1,0:T(1,128)S(1)}, u32[]{:S(2)}) copy-start(f32[16,1,256]{2,1,0:T(1,128)S(1)} %convert_element_type.87) | copy-start | bytes 49156
  47.4 122.3 %copy-start = (bf16[128,4096]{1,0:T(8,128)(2,1)S(1)}, bf16[128,4096]{1,0:T(8,128)(2,1)}, u32[]{:S(2)}) copy-start(bf16[128,4096]{1,0:T(8,128)(2,1)} %param.11) | copy-start | bytes 3145732
  47.4 125.3 %copy-start.15 = (f32[128]{0:T(128)}, f32[128]{0:T(128)S(1)}, u32[]{:S(2)}) copy-start(f32[128]{0:T(128)S(1)} %add_rsqrt_fusion) | copy-start | bytes 1540
  48.4 41.0 %copy-start.11 = (f32[128,64]{1,0:T(8,128)}, f32[128,64]{1,0:T(8,128)S(1)}, u32[]{:S(2)}) copy-start(f32[128,64]{1,0:T(8,128)S(1)} %get-tuple-element.478) | copy-start | bytes 98308
  88.8 85.1 %copy-start.7 = (bf16[128,4096]{1,0:T(8,128)(2,1)S(1)}, bf16[128,4096]{1,0:T(8,128)(2,1)}, u32[]{:S(2)}) copy-start(bf16[128,4096]{1,0:T(8,128)(2,1)} %param.13) | copy-start | bytes 3145732
  89.5 85.8 %copy-start.8 = (bf16[128,4096]{1,0:T(8,128)(2,1)S(1)}, bf16[128,4096]{1,0:T(8,128)(2,1)}, u32[]{:S(2)}) copy-start(bf16[128,4096]{1,0:T(8,128)(2,1)} %param.12) | copy-start | bytes 3145732
  173.5 382.2 %reduce-scatter.4.cloned.1.call-start = ((), (), s32[]{:S(2)}) async-start(), calls=%async_computation.6 | async-start | bytes 8912896 | tf_op jit(solution)/shard_map/reduce_scatter | solution.py:178
  267.6 1.8 copy-start.4
  272.6 1.3 copy-start.5
  278.9 1.8 copy-start.4
  283.9 1.3 copy-start.5
  290.2 1.8 copy-start.4
  295.1 1.3 copy-start.5
  301.5 1.8 copy-start.4
  306.4 1.3 copy-start.5
  449.2 106.5 %copy-start.1 = (bf16[128,4096]{1,0:T(8,128)(2,1)S(1)}, bf16[128,4096]{1,0:T(8,128)(2,1)}, u32[]{:S(2)}) copy-start(bf16[128,4096]{1,0:T(8,128)(2,1)} %param.11) | copy-start | bytes 3145732
  449.2 106.5 %copy-start.10 = (f32[16,1,256]{2,1,0:T(1,128)S(1)}, f32[16,1,256]{2,1,0:T(1,128)}, u32[]{:S(2)}) copy-start(f32[16,1,256]{2,1,0:T(1,128)} %copy-done.9) | copy-start | bytes 49156
  449.2 106.5 %copy-start.16 = (f32[128]{0:T(128)S(1)}, f32[128]{0:T(128)}, u32[]{:S(2)}) copy-start(f32[128]{0:T(128)} %copy-done.15) | copy-start | bytes 1540
  449.2 220.6 %reduce-scatter.8.cloned.1.call-start = ((), (), s32[]{:S(2)}) async-start(), calls=%async_computation.8 | async-start | bytes 8912896 | tf_op jit(solution)/shard_map/reduce_scatter | solution.py:202
  561.2 0.9 slice-start
  561.2 1.3 copy-start.12
  561.2 1.3 copy-start.13
  561.2 203.9 %reduce-scatter.6.cloned.1.call-start = ((), (), s32[]{:S(2)}) async-start(), calls=%async_computation.7 | async-start | bytes 8912896 | tf_op jit(solution)/shard_map/reduce_scatter | solution.py:201
  567.5 0.7 copy-start.17
  567.5 264.7 %all-reduce.4.cloned.1.call-start = ((), (), s32[]{:S(2)}) async-start(), calls=%async_computation.9 | async-start | bytes 2097152 | tf_op jit(solution)/shard_map/psum | solution.py:205
  569.3 4.0 copy-start.3
  571.9 2.9 copy-start.2
  572.0 2.9 copy-start.6
Sparse Core Ops, SparseCore 0:
  9.6 75.8 all-gather.4
  87.2 82.4 all-gather.6
  173.6 82.7 all-gather.8
  449.3 106.3 reduce-scatter.3
  561.4 103.2 reduce-scatter.7
  666.9 98.1 reduce-scatter.5
  767.5 64.5 all-reduce.3
where the time goes:
time: 847 us; the launch traced here: 843 us
  waiting for transfers between devices  466 us (55%)
  blocking collectives  129 us (15%)
  matrix products  95.4 us (11%)
  local copies, waits for them, and re-layouts  88.5 us (10%)
  other arithmetic  40 us (5%)
  between operations  15.2 us (2%)
    reduce_scatter x1, waiting for transfers between devices, local(): lax.psum_scatter(kv_acc, ('shard', 'ctx'), scatter_dimension=0, tiled=True)  106 us
    reduce_scatter x1, waiting for transfers between devices, local(): lax.psum_scatter(key_term, ('shard', 'ctx'), scatter_dimension=0, tiled=T...  95.3 us
    all_gather x1, waiting for transfers between devices, local(): lax.all_gather(value_weight, ('shard', 'ctx'), axis=0, tiled=True)  80.3 us
    all_gather x1, waiting for transfers between devices, local(): kv_whole = lax.all_gather(kv_local, ('shard', 'ctx'), axis=0, tiled=True)  79.8 us
    unnamed x1, blocking collectives  65.8 us
    psum x1, waiting for transfers between devices, local(): lax.psum((key_share, value_share, gain_share), 'dp')  65.5 us
    dynamic_update_slice x4, local copies, waits for them, and re-layouts, backward_step(): kv_acc = lax.dynamic_update_slice_in_dim(kv_acc, current + update, start, 0)  41.1 us
    all_gather x1, waiting for transfers between devices, local(): lax.all_gather(key_weight, ('shard', 'ctx'), axis=0, tiled=True)  37.2 us
  transfers between devices with their start and end apart: 7, of which 6 were waited for; matrix products, arithmetic and copies ran while one was open for 3% of the time, Pallas kernels for 0%

commit v1 on v0

v1 whole, which is shorter than its diff:
```python
import functools
import math

import jax
import jax.numpy as jnp
from jax import lax
from jax.experimental import pallas as pl
from jax.experimental.pallas import tpu as pltpu
from jax.sharding import PartitionSpec as P

HEAD = 128
HEADS = 4
GROUP = 8
SPAN = 64
RANKS = 16
ROWS = 128
FEATURES = 4096
SHARE = 256
WIDTH = 512
BLOCK = 272
EPSILON = 1e-05
ROPE_BASE = 500000.0
NEG_FILL = -1e30
SCALE = HEAD ** (-0.5)
EXP_SCALE = SCALE * math.log2(math.e)
MESH = pl.DeviceIdType.MESH
F32 = jnp.float32
BF16 = jnp.bfloat16
NT = (((1,), (1,)), ((), ()))


def device_at(x, core, y, z):
    return (x * 2 + core, z % 2, (z // 2) * 4 + y)


def rank_at(y, z):
    return (z % 2) * 8 + (z // 2) * 4 + y


def dot(a, b):
    return jnp.dot(a, b, preferred_element_type=F32)


def dot_nt(a, b):
    return lax.dot_general(a, b, NT, preferred_element_type=F32)


class Place:
    def __init__(self):
        dp = lax.axis_index("dp")
        shard = lax.axis_index("shard")
        ctx = lax.axis_index("ctx")
        self.x = dp // 2
        self.core = dp % 2
        self.y = ctx % 4
        self.z = (ctx // 4) * 2 + shard
        self.rank = rank_at(self.y, self.z)

    def partner(self):
        return device_at(self.x, 1 - self.core, self.y, self.z)

    def along_x(self, step):
        return device_at((self.x + step) % 4, self.core, self.y, self.z)


class Route:
    def __init__(self, place, first, send, recv):
        self.place, self.first, self.send_sems, self.recv_sems = place, first, send, recv

    def point(self, da, db):
        dy, dz = (da, db) if self.first == "y" else (db, da)
        return (self.place.y + dy + 4) % 4, (self.place.z + dz + 4) % 4

    def rank(self, da, db):
        return rank_at(*self.point(da, db))

    def device(self, da, db):
        return device_at(self.place.x, self.place.core, *self.point(da, db))

    def copy(self, index, src, dst, to):
        return pltpu.make_async_remote_copy(
            src_ref=src,
            dst_ref=dst,
            send_sem=self.send_sems.at[index],
            recv_sem=self.recv_sems.at[index],
            device_id=self.device(*to),
            device_id_type=MESH,
        )


def gather_table():
    table = [
        ((0, 0), "full", (1, 0), (-1, 0)),
        ((0, 0), "full", (-1, 0), (1, 0)),
        ((-1, 0), "lo", (1, 0), (2, 0)),
        ((1, 0), "hi", (-1, 0), (2, 0)),
    ]
    for da in (0, -1, 1, 2):
        table += [
            ((da, 0), "full", (0, 1), (da, -1)),
            ((da, 0), "full", (0, -1), (da, 1)),
            ((da, -1), "lo", (0, 1), (da, 2)),
            ((da, 1), "hi", (0, -1), (da, 2)),
        ]
    return table


class Gather(Route):
    table = gather_table()
    plan = (
        ("s0", "s1", "s4", "s5"),
        ("r0", "s2", "s8", "s9", "r1", "s3", "s12", "s13", "r4", "s6", "r5", "s7"),
        ("r2", "r3", "s16", "s17", "r8", "s10", "r9", "s11", "r12", "s14", "r13", "s15", "r6", "r7"),
        ("r16", "s18", "r17", "s19", "r10", "r11", "r14", "r15"),
        ("r18", "r19"),
    )
    whole = {0: 0, 1: 1, 3: 2, 4: 4, 5: 5, 7: 6}

    def __init__(self, place, first, slot, send, recv):
        super().__init__(place, first, send, recv)
        self.slot = slot

    def send(self, m):
        block, part, to, _ = self.table[m]
        ref = self.slot(self.rank(*block), part)
        return self.copy(m, ref, ref, to)

    def arrival(self, m):
        _, part, to, block = self.table[m]
        ref = self.slot(self.rank(*block), part)
        return self.copy(m, ref, ref, to)

    def stage(self, number, arrived=None):
        for item in self.plan[number]:
            m = int(item[1:])
            if item[0] == "s":
                self.send(m).start()
                continue
            self.arrival(m).wait_recv()
            if arrived is not None:
                _, part, _, block = self.table[m]
                if part == "full" or m in (3, 7, 11, 15, 19):
                    arrived(block)

    def drain(self):
        for m in range(20):
            self.send(m).wait_send()


class Scatter(Route):
    order = (2, 1, -1, 0)

    def __init__(self, place, first, slot, halves, wholes, send, recv):
        super().__init__(place, first, send, recv)
        self.slot, self.halves, self.wholes = slot, halves, wholes

    def message(self, m):
        if m < 16:
            i, k = m // 4, m % 4
            da = self.order[i]
            blocks = ((da, 2), (da, 2), (da, 1), (da, -1))
            to = ((0, 1), (0, -1))[k % 2]
        else:
            i, k = 4, m - 16
            blocks = ((2, 0), (2, 0), (1, 0), (-1, 0))
            to = ((1, 0), (-1, 0))[k % 2]
        part = ("lo", "hi", "full", "full")[k]
        src = self.slot(self.rank(*blocks[k]), part)
        dst = self.halves(i, part) if k < 2 else self.wholes(i, k - 2)
        return self.copy(m, src, dst, to)

    def start(self, m):
        self.message(m).start()

    def arrive(self, m):
        self.message(m).wait_recv()

    def add(self, block, part, *refs):
        ref = self.slot(self.rank(*block), part)
        total = ref[...].astype(F32)
        for other in refs:
            total = total + other[...].astype(F32)
        ref[...] = total.astype(BF16)

    def stage(self, number):
        if number == 0:
            for i in range(4):
                self.start(4 * i)
                self.start(4 * i + 1)
        elif number == 1:
            for i, da in enumerate(self.order):
                self.arrive(4 * i)
                self.add((da, 1), "lo", self.halves(i, "lo"))
                self.start(4 * i + 2)
                self.arrive(4 * i + 1)
                self.add((da, -1), "hi", self.halves(i, "hi"))
                self.start(4 * i + 3)
        elif number == 2:
            for i, da in enumerate(self.order):
                self.arrive(4 * i + 2)
                self.arrive(4 * i + 3)
                self.add((da, 0), "full", self.wholes(i, 0), self.wholes(i, 1))
                if i == 0:
                    self.start(16)
                    self.start(17)
        elif number == 3:
            self.arrive(16)
            self.add((1, 0), "lo", self.halves(4, "lo"))
            self.start(18)
            self.arrive(17)
            self.add((-1, 0), "hi", self.halves(4, "hi"))
            self.start(19)
        else:
            self.arrive(18)
            self.arrive(19)

    def total(self):
        own = self.slot(self.rank(0, 0), "full")[...].astype(F32)
        return own + self.wholes(4, 0)[...].astype(F32) + self.wholes(4, 1)[...].astype(F32)

    def drain(self):
        for m in range(20):
            self.message(m).wait_send()


def weight_rows(kind, part):
    if kind == 0:
        return {"full": pl.ds(0, 128), "lo": pl.ds(0, 64), "hi": pl.ds(64, 64)}[part]
    return {"full": pl.ds(128, 144), "lo": pl.ds(128, 64), "hi": pl.ds(192, 80)}[part]


def kernel(
    x_ref, q_ref, g_ref, spans_ref, kpos_ref, gain_ref, wk_ref, wv_ref, cos_ref, sin_ref,
    out_ref, dq_ref, dx_ref, dwk_ref, dwv_ref, dgain_ref,
    wbuf, kvbuf, qs, gs, qt, gt, probs, dscore, grads, kv_half, kv_whole, dkv, ngrad,
    terms, pair, w_half, w_whole, x_send, x_recv, x_gain, final, inv_ref,
    w_send, w_recv, hand_send, hand_recv, kv_send, kv_recv, rs_send, rs_recv,
    pair_send, pair_recv, ws_send, ws_recv, x_ssem, x_rsem,
):
    me = Place()
    barrier = pltpu.get_barrier_semaphore()
    others = [device_at(me.x, me.core, (me.y + d) % 4, me.z) for d in (1, 3)]
    others += [device_at(me.x, me.core, me.y, (me.z + d) % 4) for d in (1, 3)]
    others += [me.along_x(d) for d in (1, 2, 3)] + [me.partner()]
    for other in others:
        pl.semaphore_signal(barrier, inc=1, device_id=other, device_id_type=MESH)

    for kind, ref in ((0, wk_ref), (1, wv_ref)):
        wbuf[kind, me.rank, 0:SHARE, :] = ref[...]
        wbuf[kind, me.rank, SHARE:BLOCK, 0:SHARE] = jnp.broadcast_to(gain_ref[...], (16, SHARE))
        wbuf[kind, me.rank, SHARE:BLOCK, SHARE:WIDTH] = jnp.zeros((16, WIDTH - SHARE), BF16)
    pl.semaphore_wait(barrier, len(others))

    def hand(kind, route, block):
        index = 4 * ((block[0] + 4) % 4) + (block[1] + 4) % 4
        return pltpu.make_async_remote_copy(
            src_ref=wbuf.at[me.core, route.rank(*block), weight_rows(kind, "full")],
            dst_ref=wbuf.at[me.core, route.rank(*block), weight_rows(kind, "full")],
            send_sem=hand_send.at[kind, index],
            recv_sem=hand_recv.at[kind, index],
            device_id=me.partner(),
            device_id_type=MESH,
        )

    def handed(kind, route, block):
        index = 4 * ((block[0] + 4) % 4) + (block[1] + 4) % 4
        return pltpu.make_async_remote_copy(
            src_ref=wbuf.at[1 - me.core, route.rank(*block), weight_rows(kind, "full")],
            dst_ref=wbuf.at[1 - me.core, route.rank(*block), weight_rows(kind, "full")],
            send_sem=hand_send.at[kind, index],
            recv_sem=hand_recv.at[kind, index],
            device_id=me.partner(),
            device_id_type=MESH,
        )

    w_routes = [
        Gather(
            me,
            "yz"[kind],
            lambda rank, part, kind=kind: wbuf.at[me.core, rank, weight_rows(kind, part)],
            w_send.at[kind],
            w_recv.at[kind],
        )
        for kind in range(2)
    ]
    for route in w_routes:
        route.stage(0)

    squares = jnp.zeros((ROWS, HEAD), F32)
    for c in range(FEATURES // HEAD):
        piece = x_ref[:, c * HEAD : (c + 1) * HEAD].astype(F32)
        squares = squares + piece * piece
    inv_ref[...] = lax.rsqrt(
        jnp.sum(squares, axis=-1, keepdims=True) * (1.0 / FEATURES) + EPSILON
    )
    for number in range(1, 5):
        for kind, route in enumerate(w_routes):
            route.stage(
                number, lambda block, kind=kind, route=route: hand(kind, route, block).start()
            )
    blocks = [(a, b) for a in (0, -1, 1, 2) for b in (0, -1, 1, 2) if (a, b) != (0, 0)]
    for kind, route in enumerate(w_routes):
        for block in blocks:
            handed(kind, route, block).wait_recv()

    inverse = inv_ref[...]

    def unit_piece(r):
        return x_ref[:, pl.ds(pl.multiple_of(r * SHARE, SHARE), SHARE)].astype(F32) * inverse

    def gain_piece(r):
        return wbuf[0, r, SHARE:BLOCK, 0:SHARE].astype(F32)[0:1, :]

    def project(r, state):
        normed = (unit_piece(r) * gain_piece(r)).astype(BF16)
        return (
            state[0] + dot(normed, wbuf[0, r, 0:SHARE, :]),
            state[1] + dot(normed, wbuf[1, r, 0:SHARE, :]),
        )

    zero = jnp.zeros((ROWS, WIDTH), F32)
    key_raw, value_raw = lax.fori_loop(0, RANKS, project, (zero, zero))
    first_span = spans_ref[2 * me.rank]
    second_span = spans_ref[2 * me.rank + 1]
    flip = first_span > second_span
    low_span = jnp.minimum(first_span, second_span)
    high_span = jnp.maximum(first_span, second_span)
    cosine, sine = cos_ref[...], sin_ref[...]
    for h in range(HEADS):
        part = key_raw[:, h * HEAD : (h + 1) * HEAD]
        key = part * cosine + pltpu.roll(part, HEAD // 2, 1) * sine
        for kind, array in ((0, key), (1, value_raw[:, h * HEAD : (h + 1) * HEAD])):
            kvbuf[kind, me.rank, 0, h] = jnp.where(flip, array[SPAN:], array[:SPAN]).astype(BF16)
            kvbuf[kind, me.rank, 1, h] = jnp.where(flip, array[:SPAN], array[SPAN:]).astype(BF16)

    def kv_slot(kind, rank, part):
        ref = kvbuf.at[kind, rank]
        return {"full": ref, "lo": ref.at[0], "hi": ref.at[1]}[part]

    kv_routes = [
        Gather(
            me,
            "yz"[kind],
            lambda rank, part, kind=kind: kv_slot(kind, rank, part),
            kv_send.at[kind],
            kv_recv.at[kind],
        )
        for kind in range(2)
    ]
    for number in range(5):
        for route in kv_routes:
            route.stage(number)

    token = lax.broadcasted_iota(jnp.int32, (ROWS, 1), 0) % SPAN
    q_pos = (low_span * SPAN + token, high_span * SPAN + token)

    def scatters(h):
        def slot(kind, rank, part):
            ref = grads.at[h, kind, rank]
            return {"full": ref, "lo": ref.at[0], "hi": ref.at[1]}[part]

        return [
            Scatter(
                me,
                "yz"[kind],
                lambda rank, part, kind=kind: slot(kind, rank, part),
                lambda i, part, kind=kind: kv_half.at[h, kind, i, 0 if part == "lo" else 1],
                lambda i, side, kind=kind: kv_whole.at[h, kind, i, side],
                rs_send.at[h, kind],
                rs_recv.at[h, kind],
            )
            for kind in range(2)
        ]

    def serve(h, number):
        @pl.when(h >= 0)
        def _():
            routes = scatters(jnp.maximum(h, 0))
            for route in routes:
                route.stage(number)
            if number < 4:
                return
            for kind, route in enumerate(routes):
                total = route.total()
                low, high = total[0], total[1]
                total = jnp.concatenate(
                    [jnp.where(flip, high, low), jnp.where(flip, low, high)], axis=0
                )
                if kind == 0:
                    total = total * cos_ref[...] - pltpu.roll(total, HEAD // 2, 1) * sin_ref[...]
                else:
                    total = total * (1.0 / SCALE)
                column = pl.multiple_of(kind * WIDTH + jnp.maximum(h, 0) * HEAD, HEAD)
                dkv[:, pl.ds(column, HEAD)] = total.astype(BF16)

    def one_head(h, carry):
        for n in range(GROUP):
            column = pl.ds(pl.multiple_of((h * GROUP + n) * HEAD, HEAD), HEAD)
            for source, target in ((q_ref, qs), (g_ref, gs)):
                first, second = source[0:SPAN, column], source[SPAN:ROWS, column]
                target[0, n * SPAN : (n + 1) * SPAN, :] = jnp.where(flip, second, first)
                target[1, n * SPAN : (n + 1) * SPAN, :] = jnp.where(flip, first, second)

        def block(kind, half):
            return kvbuf[kind, :, half, h].reshape(RANKS * SPAN, HEAD)

        def tile(half, i):
            rows = pl.ds(pl.multiple_of(i * ROWS, ROWS), ROWS)
            place_rows = pl.ds(pl.multiple_of(half * WIDTH + i * ROWS, ROWS), ROWS)
            q, g = qs[half, rows, :], gs[half, rows, :]
            scores = [dot_nt(q, block(0, k)) for k in range(half + 1)]
            scores[half] = jnp.where(
                kpos_ref[half : half + 1, :] <= q_pos[half], scores[half], NEG_FILL
            )
            top = jnp.max(scores[0], axis=-1, keepdims=True)
            if half:
                top = jnp.maximum(top, jnp.max(scores[1], axis=-1, keepdims=True))
            weights = [jnp.exp2((s - top) * EXP_SCALE) for s in scores]
            total = jnp.sum(weights[0], axis=-1, keepdims=True)
            if half:
                total = total + jnp.sum(weights[1], axis=-1, keepdims=True)
            low = [w.astype(BF16) for w in weights]
            attended = dot(low[0], block(1, 0))
            if half:
                attended = attended + dot(low[1], block(1, 1))
            share = 1.0 / total
            attended = (attended * share).astype(BF16)
            grad = (g.astype(F32) * (share * SCALE)).astype(BF16)
            grad_f = grad.astype(F32)
            row_dot = jnp.sum(grad_f * attended.astype(F32), axis=-1, keepdims=True)
            gt[:, place_rows] = jnp.transpose(grad_f).astype(BF16)
            qt[:, place_rows] = jnp.transpose(q.astype(F32)).astype(BF16)
            back = None
            for k in range(half + 1):
                dots = dot_nt(grad, block(1, k))
                ds = (weights[k] * (dots - row_dot)).astype(BF16)
                target = rows if k else place_rows
                probs[k, target, :] = low[k]
                dscore[k, target, :] = ds
                term = dot(ds, block(0, k))
                back = term if back is None else back + term
            qs[half, rows, :] = back.astype(BF16)
            gs[half, rows, :] = attended

        def tiles(half, start, stop):
            def body(i, inner):
                tile(half, i)
                return inner

            lax.fori_loop(start, stop, body, 0)

        serve(h - 1, 1)
        tiles(0, 0, 4)
        serve(h - 1, 2)
        tiles(1, 0, 2)
        serve(h - 1, 3)
        tiles(1, 2, 4)
        serve(h - 1, 4)
        for kind, left, right in ((0, qt, dscore), (1, gt, probs)):
            low = dot(left[...], right[0])
            high = dot(left[:, WIDTH:], right[1, 0:WIDTH, :])
            for half, array in ((0, low), (1, high)):
                grads[h, kind, :, half] = (
                    jnp.transpose(array).astype(BF16).reshape(RANKS, SPAN, HEAD)
                )
        for route in scatters(h):
            route.stage(0)
        for n in range(GROUP):
            column = pl.ds(pl.multiple_of((h * GROUP + n) * HEAD, HEAD), HEAD)
            for source, target in ((qs, dq_ref), (gs, out_ref)):
                low = source[0, n * SPAN : (n + 1) * SPAN, :]
                high = source[1, n * SPAN : (n + 1) * SPAN, :]
                target[0:SPAN, column] = jnp.where(flip, high, low)
                target[SPAN:ROWS, column] = jnp.where(flip, low, high)
        return carry

    lax.fori_loop(0, HEADS, one_head, 0)
    for number in range(1, 5):
        serve(jnp.int32(HEADS - 1), number)

    def pair_copy(r):
        return pltpu.make_async_remote_copy(
            src_ref=terms.at[1 - me.core, r],
            dst_ref=pair.at[r],
            send_sem=pair_send.at[r],
            recv_sem=pair_recv.at[r],
            device_id=me.partner(),
            device_id_type=MESH,
        )

    def weight_terms(r, mean):
        unit = unit_piece(r)
        gain = gain_piece(r)
        normed_t = jnp.transpose(unit * gain).astype(BF16)
        dk, dv = dkv[:, 0:WIDTH], dkv[:, WIDTH:]
        terms[0, r, 0:SHARE, :] = dot(normed_t, dk).astype(BF16)
        terms[1, r, 0:SHARE, :] = dot(normed_t, dv).astype(BF16)
        normed_grad = dot_nt(dk, wbuf[0, r, 0:SHARE, :]) + dot_nt(dv, wbuf[1, r, 0:SHARE, :])
        gain_term = jnp.sum(unit * normed_grad, axis=0, keepdims=True)
        for kind in range(2):
            terms[kind, r, SHARE:BLOCK, 0:SHARE] = jnp.broadcast_to(
                gain_term, (16, SHARE)
            ).astype(BF16)
            terms[kind, r, SHARE:BLOCK, SHARE:WIDTH] = jnp.zeros((16, WIDTH - SHARE), BF16)
        pair_copy(r).start()
        unit_grad = normed_grad * gain
        ngrad[:, pl.ds(pl.multiple_of(r * SHARE, SHARE), SHARE)] = unit_grad
        return mean + jnp.sum(unit_grad * unit, axis=-1, keepdims=True)

    mean = lax.fori_loop(0, RANKS, weight_terms, jnp.zeros((ROWS, 1), F32))
    mean = mean * (1.0 / FEATURES)

    def pair_sum(r, carry):
        pair_copy(r).wait()
        terms[me.core, r] = (terms[me.core, r].astype(F32) + pair[r].astype(F32)).astype(BF16)
        return carry

    lax.fori_loop(0, RANKS, pair_sum, 0)

    def half_rows(kind, part):
        return pl.ds(0, 80 if (kind and part == "hi") else 64)

    w_scatters = [
        Scatter(
            me,
            "yz"[kind],
            lambda rank, part, kind=kind: terms.at[me.core, rank, weight_rows(kind, part)],
            lambda i, part, kind=kind: w_half.at[
                kind, i, 0 if part == "lo" else 1, half_rows(kind, part)
            ],
            lambda i, side, kind=kind: w_whole.at[kind, i, side, pl.ds(0, 144 if kind else 128)],
            ws_send.at[kind],
            ws_recv.at[kind],
        )
        for kind in range(2)
    ]
    for route in w_scatters:
        route.stage(0)

    def row_grad(r, carry):
        columns = pl.ds(pl.multiple_of(r * SHARE, SHARE), SHARE)
        dx_ref[:, columns] = (
            inv_ref[...] * (ngrad[:, columns] - unit_piece(r) * mean)
        ).astype(BF16)
        return carry

    lax.fori_loop(0, RANKS, row_grad, 0)
    for number in range(1, 5):
        for route in w_scatters:
            route.stage(number)

    for kind, route in enumerate(w_scatters):
        x_send[128 * kind : 128 * kind + (144 if kind else 128), :] = route.total().astype(BF16)

    def quarter(number):
        return pl.ds(pl.multiple_of(number * 64, 64), 64)

    def x_copy(index, src, dst, to):
        return pltpu.make_async_remote_copy(
            src_ref=src,
            dst_ref=dst,
            send_sem=x_ssem.at[index],
            recv_sem=x_rsem.at[index],
            device_id=to,
            device_id_type=MESH,
        )

    sums = [
        x_copy(d - 1, x_send.at[quarter((me.x + d) % 4)], x_recv.at[d - 1], me.along_x(d))
        for d in (1, 2, 3)
    ]
    gains = [
        x_copy(d + 2, x_send.at[pl.ds(SHARE, 16)], x_gain.at[d - 1], me.along_x(d))
        for d in (1, 2, 3)
    ]
    for copy in sums + gains:
        copy.start()
    for copy in sums:
        copy.wait_recv()
    total = x_send[quarter(me.x), :].astype(F32)
    for d in range(3):
        total = total + x_recv[d].astype(F32)
    final[me.core, quarter(me.x), :] = total.astype(BF16)
    mine = final.at[me.core, quarter(me.x)]
    spread = [x_copy(5 + d, mine, mine, me.along_x(d)) for d in (1, 2, 3)]
    for copy in spread:
        copy.start()
    for copy in gains:
        copy.wait_recv()
    total = x_send[SHARE:BLOCK, :].astype(F32)
    for d in range(3):
        total = total + x_gain[d].astype(F32)
    dgain_ref[...] = total[0:8, 0:SHARE]
    for d in (1, 2, 3):
        theirs = final.at[me.core, quarter((me.x + 4 - d) % 4)]
        x_copy(5 + d, theirs, theirs, me.along_x(d)).wait_recv()
    last = x_copy(9, final.at[me.core], final.at[me.core], me.partner())
    last.start()
    x_copy(9, final.at[1 - me.core], final.at[1 - me.core], me.partner()).wait_recv()
    dwk_ref[...] = final[0].astype(F32)
    dwv_ref[...] = final[1].astype(F32)

    for kind, route in enumerate(w_routes):
        route.drain()
        for block in blocks:
            hand(kind, route, block).wait_send()
    for route in kv_routes:
        route.drain()

    def drain_head(h, carry):
        for route in scatters(h):
            route.drain()
        return carry

    lax.fori_loop(0, HEADS, drain_head, 0)
    for route in w_scatters:
        route.drain()
    for copy in sums + gains + spread + [last]:
        copy.wait_send()


def local(inputs, queries, out_grad, span_ids, norm_gain, key_weight, value_weight):
    rank = lax.axis_index("shard") * 8 + lax.axis_index("ctx")
    spans = span_ids.reshape(RANKS, 2)
    own = lax.dynamic_slice_in_dim(spans, rank, 1, 0).reshape(2, 1)
    token = jnp.arange(SPAN, dtype=jnp.int32)[None, :]
    own_pos = (own * SPAN + token).reshape(ROWS)
    low = jnp.minimum(spans[:, 0], spans[:, 1])[:, None] * SPAN + token
    high = jnp.maximum(spans[:, 0], spans[:, 1])[:, None] * SPAN + token
    kpos = jnp.stack([low.reshape(-1), high.reshape(-1)])
    half = HEAD // 2
    frequency = jnp.exp(
        -math.log(ROPE_BASE) * (2.0 * jnp.arange(half, dtype=jnp.float32) / HEAD)
    )
    angles = own_pos.astype(jnp.float32)[:, None] * frequency[None, :]
    cosine, sine = jnp.cos(angles), jnp.sin(angles)
    cosine = jnp.concatenate([cosine, cosine], axis=1)
    sine = jnp.concatenate([-sine, sine], axis=1)

    vmem = pl.BlockSpec(memory_space=pltpu.VMEM)
    smem = pl.BlockSpec(memory_space=pltpu.SMEM)
    dma = pltpu.SemaphoreType.DMA
    outs = pl.pallas_call(
        kernel,
        out_shape=[
            jax.ShapeDtypeStruct((ROWS, FEATURES), BF16),
            jax.ShapeDtypeStruct((ROWS, FEATURES), BF16),
            jax.ShapeDtypeStruct((ROWS, FEATURES), BF16),
            jax.ShapeDtypeStruct((SHARE, WIDTH), F32),
            jax.ShapeDtypeStruct((SHARE, WIDTH), F32),
            jax.ShapeDtypeStruct((8, SHARE), F32),
        ],
        in_specs=[vmem, vmem, vmem, smem] + [vmem] * 6,
        out_specs=[vmem] * 6,
        scratch_shapes=[
            pltpu.VMEM((2, RANKS, BLOCK, WIDTH), BF16),
            pltpu.VMEM((2, RANKS, 2, HEADS, SPAN, HEAD), BF16),
            pltpu.VMEM((2, WIDTH, HEAD), BF16),
            pltpu.VMEM((2, WIDTH, HEAD), BF16),
            pltpu.VMEM((HEAD, 2 * WIDTH), BF16),
            pltpu.VMEM((HEAD, 2 * WIDTH), BF16),
            pltpu.VMEM((2, 2 * WIDTH, RANKS * SPAN), BF16),
            pltpu.VMEM((2, 2 * WIDTH, RANKS * SPAN), BF16),
            pltpu.VMEM((HEADS, 2, RANKS, 2, SPAN, HEAD), BF16),
            pltpu.VMEM((HEADS, 2, 5, 2, SPAN, HEAD), BF16),
            pltpu.VMEM((HEADS, 2, 5, 2, 2, SPAN, HEAD), BF16),
            pltpu.VMEM((ROWS, 2 * WIDTH), BF16),
            pltpu.VMEM((ROWS, FEATURES), F32),
            pltpu.VMEM((2, RANKS, BLOCK, WIDTH), BF16),
            pltpu.VMEM((RANKS, BLOCK, WIDTH), BF16),
            pltpu.VMEM((2, 5, 2, 80, WIDTH), BF16),
            pltpu.VMEM((2, 5, 2, 144, WIDTH), BF16),
            pltpu.VMEM((BLOCK, WIDTH), BF16),
            pltpu.VMEM((3, 64, WIDTH), BF16),
            pltpu.VMEM((3, 16, WIDTH), BF16),
            pltpu.VMEM((2, SHARE, WIDTH), BF16),
            pltpu.VMEM((ROWS, 1), F32),
            dma((2, 20)), dma((2, 20)),
            dma((2, 16)), dma((2, 16)),
            dma((2, 20)), dma((2, 20)),
            dma((HEADS, 2, 20)), dma((HEADS, 2, 20)),
            dma((RANKS,)), dma((RANKS,)),
            dma((2, 20)), dma((2, 20)),
            dma((10,)), dma((10,)),
        ],
        compiler_params=pltpu.CompilerParams(
            collective_id=0, has_side_effects=True, vmem_limit_bytes=60 * 1024 * 1024
        ),
        cost_estimate=pl.CostEstimate(
            flops=12 * 10**9, bytes_accessed=10**7, transcendentals=7 * 10**6
        ),
        name="layer",
    )(
        inputs, queries, out_grad, spans.reshape(-1), kpos, norm_gain.reshape(1, SHARE),
        key_weight, value_weight, cosine, sine,
    )
    return (*outs[:5], outs[5][0])


def solution(mesh):
    tokens = P(("dp", "shard", "ctx"), None)
    rows = P(("shard", "ctx"), None)
    return jax.shard_map(
        local,
        mesh=mesh,
        in_specs=(tokens, tokens, tokens, P("dp", None, None), P(("shard", "ctx")), rows, rows),
        out_specs=(tokens, tokens, tokens, rows, rows, P(("shard", "ctx"))),
        check_vma=False,
    )
```

time: 847 us -> 216 us (0.26)
  waiting for transfers between devices: 466 us -> 0 us
  Pallas kernels: 0 us -> 202 us
  blocking collectives: 129 us -> 0 us
  matrix products: 95.4 us -> 0 us
  local copies, waits for them, and re-layouts: 88.5 us -> 11.5 us
  other arithmetic: 40 us -> 2.02 us
  between operations: 15.2 us -> 0.68 us
    pallas_call x0 -> x1, Pallas kernels: none -> 202 us  [local(): pl.pallas_call(kernel, out_shape=[jax.ShapeDtypeStruct((ROWS, FEATURES),...]
    reduce_scatter x3 -> x0, waiting for transfers between devices: 202 us -> none  [the longest x1 106 us: local(): lax.psum_scatter(kv_acc, ('shard', 'ctx'), scatter_dimension=0, tiled=True)]
    all_gather x3 -> x0, waiting for transfers between devices: 197 us -> none  [the longest x1 80.3 us: local(): lax.all_gather(value_weight, ('shard', 'ctx'), axis=0, tiled=True)]
    dot_general x34 -> x0, matrix products: 95.4 us -> none  [the longest x4 17.7 us: backward_step(): jnp.einsum('tkgd,nkd->kgtn', grouped_g, value_part, preferred_element_typ...]
    unnamed x1 -> x0, blocking collectives: 65.8 us -> none
    psum x1 -> x0, waiting for transfers between devices: 65.5 us -> none  [local(): lax.psum((key_share, value_share, gain_share), 'dp')]
    dynamic_update_slice x4 -> x0, local copies, waits for them, and re-layouts: 41.1 us -> none  [backward_step(): kv_acc = lax.dynamic_update_slice_in_dim(kv_acc, current + update, start, 0)]
    all_gather x1 -> x0, blocking collectives: 35.5 us -> none  [local(): lax.all_gather(norm_gain, ('shard', 'ctx'), axis=0, tiled=True)]
  transfers between devices with their start and end apart: 7 -> 0, of which waited for: 6 -> 0; matrix products, arithmetic and copies ran while one was open for 3% -> 0% of each run, Pallas kernels for 0% -> 0%
where the time goes in v1:
time: 216 us
  Pallas kernels  202 us (94%)
  local copies, waits for them, and re-layouts  11.5 us (5%)
    pallas_call x1, Pallas kernels, local(): pl.pallas_call(kernel, out_shape=[jax.ShapeDtypeStruct((ROWS, FEATURES),...  202 us
    unnamed x18, local copies, waits for them, and re-layouts  8.8 us

profile of v1, /device:TPU:1, one launch (start us, length us, event | category | flops | bytes accessed | tf_op | source)
XLA Modules:
  0.0 216.1 jit_solution(3378406123376206533)
XLA Ops:
  0.6 0.0 copy-start.4
  0.6 0.7 copy-done.4
  1.3 0.2 multiply_reduce_fusion
  1.5 0.1 add_convert_fusion
  1.6 0.1 convert_element_type.11
  1.7 0.0 copy-start.5
  1.7 0.6 copy-done.5
  2.3 0.6 reshape.97.gain_ref
  2.9 0.1 copy.14
  3.0 0.6 reshape_reshape.3.spans_ref
  3.6 0.1 iota_add_fusion
  3.6 0.1 add.84
  3.7 0.1 add.79
  3.8 0.6 pad_add_fusion.kpos_ref
  4.4 0.3 fusion
  4.7 0.8 pad_maximum_fusion
  5.5 201.9 %layer.1 = (bf16[128,4096]{1,0:T(8,128)(2,1)}, bf16[128,4096]{1,0:T(8,128)(2,1)}, bf16[128,4096]{1,0:T(8,128)(2,1)}, f32[256,512]{1,0:T(8,128)}, f32[256,512]{1,0:T(8,128)}, /*index=5*/f32[8,256]{1,0:T(8,128)}) custom-call(bf16[128,4096]{1,0:T(8,128)(2,1)} %x_ref.1, bf16[128,4096]{1,0:T(8,128)(2,1)} %q_ref.1, bf16[128,4096]{1,0:T(8,128)(2,1)} %g_ref.1, ...), custom_call_target="tpu_custom_call" | custom-call | flops 12000000000 | bytes 10000000 | tf_op jit(solution)/shard_map/layer/pallas_call | solution.py:643
  207.4 1.3 slice.13
  208.7 0.0 copy-start.1
  208.7 2.4 %copy.20 = bf16[128,4096]{1,0:T(8,128)(2,1)} copy(bf16[128,4096]{1,0:T(8,128)(2,1)} %get-tuple-element.33) | data formatting | bytes 2097152
  211.1 0.0 copy-done.1
  211.1 0.0 copy-start
  211.1 1.0 copy.21
  212.0 0.6 copy-done
  212.7 0.0 copy-start.3
  212.7 1.0 copy.22
  213.7 0.4 copy-done.3
  214.1 0.0 copy-start.2
  214.1 0.8 copy.23
  214.9 0.4 copy-done.2
  215.3 0.8 copy.24
  (2 shorter events, 0.0 us)
Async XLA Ops:
  0.6 0.7 copy-start.4
  1.7 0.7 copy-start.5
  208.7 2.4 %copy-start.1 = (bf16[128,4096]{1,0:T(8,128)(2,1)S(1)}, bf16[128,4096]{1,0:T(8,128)(2,1)}, u32[]{:S(2)}) copy-start(bf16[128,4096]{1,0:T(8,128)(2,1)} %get-tuple-element.34) | copy-start | bytes 3145732
  211.1 1.6 copy-start
  212.7 1.4 copy-start.3
  214.1 1.2 copy-start.2

commit v2 on v0

v2 whole, which is shorter than its diff:
```python
import functools
import math

import jax
import jax.numpy as jnp
from jax import lax
from jax.experimental import pallas as pl
from jax.experimental.pallas import tpu as pltpu
from jax.sharding import PartitionSpec as P

HEAD = 128
HEADS = 4
GROUP = 8
SPAN = 64
RANKS = 16
ROWS = 128
FEATURES = 4096
SHARE = 256
WIDTH = 512
BLOCK = 144
PART = 128
EARLY = 2
EPSILON = 1e-05
ROPE_BASE = 500000.0
NEG_FILL = -1e30
SCALE = HEAD ** (-0.5)
EXP_SCALE = SCALE * math.log2(math.e)
MESH = pl.DeviceIdType.MESH
F32 = jnp.float32
BF16 = jnp.bfloat16
NT = (((1,), (1,)), ((), ()))


def device_at(x, core, y, z):
    return (x * 2 + core, z % 2, (z // 2) * 4 + y)


def rank_at(y, z):
    return (z % 2) * 8 + (z // 2) * 4 + y


def dot(a, b):
    return jnp.dot(a, b, preferred_element_type=F32)


def dot_nt(a, b):
    return lax.dot_general(a, b, NT, preferred_element_type=F32)


class Place:
    def __init__(self):
        dp = lax.axis_index("dp")
        shard = lax.axis_index("shard")
        ctx = lax.axis_index("ctx")
        self.x = dp // 2
        self.core = dp % 2
        self.y = ctx % 4
        self.z = (ctx // 4) * 2 + shard
        self.rank = rank_at(self.y, self.z)

    def partner(self):
        return device_at(self.x, 1 - self.core, self.y, self.z)

    def along_x(self, step):
        return device_at((self.x + step) % 4, self.core, self.y, self.z)


STEPS = (1, 3, 2)


def start_all(copies):
    for copy in copies:
        copy.start()


def add_into(ref, others):
    total = ref[...].astype(F32)
    for other in others:
        total = total + other[...].astype(F32)
    ref[...] = total.astype(BF16)


class Route:
    def __init__(self, place, kind, slot, send, recv):
        self.place, self.kind, self.slot = place, kind, slot
        self.send_sems, self.recv_sems = send, recv
        self.a, self.b = (place.z, place.y) if kind else (place.y, place.z)

    def block(self, da, db):
        a, b = (self.a + da) % 4, (self.b + db) % 4
        return self.slot(a, b) if self.kind else self.slot(b, a)

    def column(self, db):
        b = (self.b + db) % 4
        return self.slot(slice(None), b) if self.kind else self.slot(b, slice(None))

    def device(self, da, db):
        a, b = (self.a + da) % 4, (self.b + db) % 4
        y, z = (b, a) if self.kind else (a, b)
        return device_at(self.place.x, self.place.core, y, z)

    def copy(self, index, src, dst, to):
        return pltpu.make_async_remote_copy(
            src_ref=src,
            dst_ref=dst,
            send_sem=self.send_sems.at[index],
            recv_sem=self.recv_sems.at[index],
            device_id=to,
            device_id_type=MESH,
        )

    def drain(self):
        for n in range(6):
            self.message(n).wait_send()


class Gather(Route):
    def message(self, n, back=False):
        step = STEPS[n % 3]
        if n < 3:
            ref = self.block(4 - step if back else 0, 0)
            return self.copy(n, ref, ref, self.device(step, 0))
        ref = self.column(4 - step if back else 0)
        return self.copy(n, ref, ref, self.device(0, step))

    def stage(self, number, arrived=None):
        if number == 0:
            start_all([self.message(n) for n in range(3)])
        elif number == 1:
            for n in range(3):
                self.message(n, True).wait_recv()
            start_all([self.message(n) for n in range(3, 6)])
            if arrived is not None:
                arrived(0)
        else:
            for n in range(3, 6):
                self.message(n, True).wait_recv()
                if arrived is not None:
                    arrived(4 - STEPS[n - 3])


class Scatter(Route):
    def __init__(self, place, kind, slot, columns, blocks, send, recv):
        super().__init__(place, kind, slot, send, recv)
        self.columns, self.blocks = columns, blocks

    def message(self, n):
        step = STEPS[n % 3]
        if n < 3:
            return self.copy(n, self.column(step), self.columns(n), self.device(0, step))
        return self.copy(n, self.block(step, 0), self.blocks(n - 3), self.device(step, 0))

    def stage(self, number):
        if number == 0:
            start_all([self.message(n) for n in range(3)])
        elif number == 1:
            for n in range(3):
                self.message(n).wait_recv()
            for n, step in enumerate(STEPS + (0,)):
                place = (self.a + step) % 4
                add_into(self.block(step, 0), [self.columns(i).at[place] for i in range(3)])
                if step:
                    self.message(3 + n).start()
        else:
            for n in range(3, 6):
                self.message(n).wait_recv()

    def total(self):
        total = self.block(0, 0)[...].astype(F32)
        for n in range(3):
            total = total + self.blocks(n)[...].astype(F32)
        return total


class Ring(Route):
    def __init__(self, place, slot, send, recv, landing=None):
        self.place, self.slot, self.send_sems, self.recv_sems = place, slot, send, recv
        self.landing = landing

    def own(self, step):
        return self.slot((self.place.x + step) % 4)

    def drain(self):
        for n in range(3):
            self.message(n).wait_send()


class RingGather(Ring):
    def message(self, n, back=False):
        ref = self.own(4 - STEPS[n] if back else 0)
        return self.copy(n, ref, ref, self.place.along_x(STEPS[n]))

    def stage(self, number):
        if number == 0:
            start_all([self.message(n) for n in range(3)])
        else:
            for n in range(3):
                self.message(n, True).wait_recv()


class RingScatter(Ring):
    def message(self, n):
        return self.copy(n, self.own(STEPS[n]), self.landing(n), self.place.along_x(STEPS[n]))

    def stage(self, number):
        if number == 0:
            start_all([self.message(n) for n in range(3)])
        else:
            for n in range(3):
                self.message(n).wait_recv()
            add_into(self.own(0), [self.landing(n) for n in range(3)])


def tall_rows(kind, with_gain):
    return pl.ds(64, 80 if with_gain else 64) if kind else pl.ds(0, 64)


def piece_rows(number):
    return pl.ds(pl.multiple_of(number * 32, 32), 32)


def kernel(
    x_hbm, q_hbm, g_hbm, spans_ref, kpos_ref, gain_ref, wk_ref, wv_ref, cos_ref, sin_ref,
    out_hbm, dq_hbm, dx_hbm, dwk_ref, dwv_ref, dgain_ref,
    x_ref, q_ref, g_ref, w_first, w_rest, kvbuf, qs, gs, qt, gt, probs_low, probs_high, ds_low, ds_high,
    grads, kv_columns, kv_blocks, dkv, ngrad, normed_t, t_last, p_last, p_rest, q_columns, q_blocks,
    w_columns, w_blocks, r_land, l_land, x_send, x_gain, final, inv_ref,
    io_sem, w_send, w_recv, hand_send, hand_recv, wx_send, wx_recv, kv_send, kv_recv,
    rs_send, rs_recv, pair_send, pair_recv, ws_send, ws_recv, xr_send, xr_recv, x_ssem, x_rsem,
):
    me = Place()

    def wref(h):
        return w_rest.at[h - 1] if h else w_first

    def tref(h):
        return wref(h) if h < HEADS - 1 else t_last

    def pref(h):
        return p_rest.at[h] if h < HEADS - 1 else p_last

    barrier = pltpu.get_barrier_semaphore()
    loads = [
        pltpu.make_async_copy(src, dst, io_sem.at[n])
        for n, (src, dst) in enumerate(((x_hbm, x_ref), (q_hbm, q_ref), (g_hbm, g_ref)))
    ]
    for copy in loads:
        copy.start()

    for h in range(HEADS):
        columns = slice(h * HEAD, (h + 1) * HEAD)
        for part in range(2):
            rows = slice(part * PART, (part + 1) * PART)
            wref(h)[me.z, me.y, part, 0:PART, 0:HEAD] = wk_ref[rows, columns]
            wref(h)[me.z, me.y, part, 0:PART, HEAD : 2 * HEAD] = wv_ref[rows, columns]
    for part in range(2):
        w_first[me.z, me.y, part, PART:BLOCK, :] = jnp.broadcast_to(gain_ref[...], (16, SHARE))

    others = [device_at(me.x, me.core, (me.y + d) % 4, me.z) for d in (1, 2, 3)]
    others += [device_at(me.x, me.core, me.y, (me.z + d) % 4) for d in (1, 2, 3)]
    others += [me.along_x(d) for d in (1, 2, 3)] + [me.partner()]
    for other in others:
        pl.semaphore_signal(barrier, inc=1, device_id=other, device_id_type=MESH)
    pl.semaphore_wait(barrier, len(others))

    w_routes = [
        [
            Gather(
                me,
                kind,
                lambda z, y, h=h, kind=kind: wref(h).at[z, y, me.core, tall_rows(kind, h == 0)],
                w_send.at[h, kind],
                w_recv.at[h, kind],
            )
            for kind in range(2)
        ]
        for h in range(EARLY)
    ]

    late_routes = [
        Gather(
            me,
            kind,
            lambda z, y, kind=kind: w_rest.at[
                pl.ds(EARLY - 1, HEADS - EARLY), z, y, me.core, piece_rows(me.x), pl.ds(kind * HEAD, HEAD)
            ],
            w_send.at[EARLY, kind],
            w_recv.at[EARLY, kind],
        )
        for kind in range(2)
    ]
    for route in late_routes:
        route.column = lambda db, route=route: w_rest.at[
            (pl.ds(EARLY - 1, HEADS - EARLY),)
            + ((slice(None), (route.b + db) % 4) if route.kind else ((route.b + db) % 4, slice(None)))
            + (me.core, piece_rows(me.x), pl.ds(route.kind * HEAD, HEAD))
        ]
    wx = {
        h: RingGather(
            me,
            lambda number, h=h: wref(h).at[:, :, me.core, piece_rows(number)],
            wx_send.at[h - EARLY],
            wx_recv.at[h - EARLY],
        )
        for h in range(EARLY, HEADS)
    }

    def hand_copy(index, ref):
        return pltpu.make_async_remote_copy(
            src_ref=ref,
            dst_ref=ref,
            send_sem=hand_send.at[index],
            recv_sem=hand_recv.at[index],
            device_id=me.partner(),
            device_id_type=MESH,
        )

    def hand_column(core, kind, db):
        b = (w_routes[0][kind].b + db) % 4
        z, y = (slice(None), b) if kind else (b, slice(None))
        return hand_copy(4 * kind + db, w_first.at[z, y, core, tall_rows(kind, True)])

    def hand_head(core, h):
        return hand_copy(7 + h, wref(h).at[:, :, core])

    def w_stage(h, number):
        for kind, route in enumerate(w_routes[h]):
            if h:
                route.stage(number)
            else:
                route.stage(number, lambda db, kind=kind: hand_column(me.core, kind, db).start())
        if h and number == 2:
            hand_head(me.core, h).start()

    def late_stage(number):
        for route in late_routes:
            route.stage(number)

    kv_routes = [
        [
            Gather(
                me,
                kind,
                lambda z, y, h=h, kind=kind: kvbuf.at[h, kind, z, y],
                kv_send.at[h, kind],
                kv_recv.at[h, kind],
            )
            for kind in range(2)
        ]
        for h in range(HEADS)
    ]

    def kv_stage(h, number):
        for route in kv_routes[h]:
            route.stage(number)

    rs_routes = [
        [
            Scatter(
                me,
                kind,
                lambda z, y, h=h, kind=kind: grads.at[h, kind, z, y],
                lambda n, h=h, kind=kind: kv_columns.at[h, kind, n],
                lambda n, h=h, kind=kind: kv_blocks.at[h, kind, n],
                rs_send.at[h, kind],
                rs_recv.at[h, kind],
            )
            for kind in range(2)
        ]
        for h in range(HEADS)
    ]

    first_span = spans_ref[2 * me.rank]
    second_span = spans_ref[2 * me.rank + 1]
    flip = first_span > second_span
    low_span = jnp.minimum(first_span, second_span)
    high_span = jnp.maximum(first_span, second_span)

    def rs_stage(h, number):
        for kind, route in enumerate(rs_routes[h]):
            route.stage(number)
            if number < 2:
                continue
            total = route.total()
            low, high = total[0], total[1]
            total = jnp.concatenate(
                [jnp.where(flip, high, low), jnp.where(flip, low, high)], axis=0
            )
            if kind == 0:
                total = total * cos_ref[...] - pltpu.roll(total, HEAD // 2, 1) * sin_ref[...]
            else:
                total = total * (1.0 / SCALE)
            dkv[h, :, kind * HEAD : (kind + 1) * HEAD] = total.astype(BF16)

    def term_rows(h):
        return pl.ds(0, BLOCK if h == HEADS - 1 else PART)

    def pair_copy(h, j):
        return pltpu.make_async_remote_copy(
            src_ref=tref(h).at[j, :, 1 - me.core, term_rows(h)],
            dst_ref=pref(h).at[j],
            send_sem=pair_send.at[h, j],
            recv_sem=pair_recv.at[h, j],
            device_id=me.partner(),
            device_id_type=MESH,
        )

    def pair_sum(h):
        def group(j, carry):
            pair_copy(h, j).wait_recv()

            def one(n, inner):
                add_into(tref(h).at[j, n, me.core, term_rows(h)], [pref(h).at[j, n]])
                return inner

            lax.fori_loop(0, 4, one, 0)
            return carry

        lax.fori_loop(0, 4, group, 0)

    xr_routes = [
        RingScatter(
            me,
            lambda number, h=h: tref(h).at[:, :, me.core, piece_rows(number)],
            xr_send.at[h],
            xr_recv.at[h],
            lambda n, h=h: r_land.at[h, n],
        )
        for h in range(HEADS - 1)
    ]
    xr_routes.append(
        RingScatter(
            me,
            lambda number: x_send.at[piece_rows(number)],
            xr_send.at[HEADS - 1],
            xr_recv.at[HEADS - 1],
            lambda n: l_land.at[n],
        )
    )
    ws_routes = [
        [
            Scatter(
                me,
                kind,
                lambda z, y, h=h, kind=kind: tref(h).at[
                    z, y, me.core, piece_rows(me.x), pl.ds(kind * HEAD, HEAD)
                ],
                lambda n, h=h, kind=kind: q_columns.at[h, kind, n],
                lambda n, h=h, kind=kind: q_blocks.at[h, kind, n],
                ws_send.at[h, kind],
                ws_recv.at[h, kind],
            )
            for kind in range(2)
        ]
        for h in range(HEADS - 1)
    ]
    ws_routes.append(
        [
            Scatter(
                me,
                kind,
                lambda z, y, kind=kind: t_last.at[z, y, me.core, tall_rows(kind, True)],
                lambda n, kind=kind: w_columns.at[kind, n, :, pl.ds(0, 80 if kind else 64)],
                lambda n, kind=kind: w_blocks.at[kind, n, pl.ds(0, 80 if kind else 64)],
                ws_send.at[HEADS - 1, kind],
                ws_recv.at[HEADS - 1, kind],
            )
            for kind in range(2)
        ]
    )

    def xr_stage(h, number):
        xr_routes[h].stage(number)

    def ws_stage(h, number):
        for kind, route in enumerate(ws_routes[h]):
            route.stage(number)
            if number < 2:
                continue
            total = route.total().astype(BF16)
            if h < HEADS - 1:
                final[
                    me.core, h, piece_rows(me.x), kind * HEAD : (kind + 1) * HEAD
                ] = total
            else:
                x_send[64 * kind : 64 * kind + (80 if kind else 64), :] = total

    def columns_of(r):
        return pl.ds(pl.multiple_of(rank_at(r % 4, r // 4) * SHARE, SHARE), SHARE)

    def unit_piece(r):
        return x_ref[:, columns_of(r)].astype(F32) * inv_ref[...]

    def gain_piece(r):
        return w_first[r // 4, r % 4, 0, PART:BLOCK, :].astype(F32)[0:1, :]

    def weight_block(h, r):
        return wref(h)[r // 4, r % 4, :, 0:PART, :].reshape(SHARE, 2 * HEAD)

    def normalise():
        squares = jnp.zeros((ROWS, HEAD), F32)
        for c in range(FEATURES // HEAD):
            piece = x_ref[:, c * HEAD : (c + 1) * HEAD].astype(F32)
            squares = squares + piece * piece
        inv_ref[...] = lax.rsqrt(
            jnp.sum(squares, axis=-1, keepdims=True) * (1.0 / FEATURES) + EPSILON
        )

    def normed_piece(r):
        return unit_piece(r) * gain_piece(r)

    def turn():
        def one(r, carry):
            normed_t[r] = jnp.transpose(normed_piece(r)).astype(BF16)
            return carry

        lax.fori_loop(0, RANKS, one, 0)

    def project(h):
        raw = lax.fori_loop(
            0,
            RANKS,
            lambda r, total: total + dot(normed_piece(r).astype(BF16), weight_block(h, r)),
            jnp.zeros((ROWS, 2 * HEAD), F32),
        )
        key = raw[:, 0:HEAD]
        key = key * cos_ref[...] + pltpu.roll(key, HEAD // 2, 1) * sin_ref[...]
        for kind, array in ((0, key), (1, raw[:, HEAD:])):
            kvbuf[h, kind, me.z, me.y, 0] = jnp.where(flip, array[SPAN:], array[:SPAN]).astype(BF16)
            kvbuf[h, kind, me.z, me.y, 1] = jnp.where(flip, array[:SPAN], array[SPAN:]).astype(BF16)

    def weight_terms(h):
        last = h == HEADS - 1

        def one(j, n, mean):
            r = 4 * j + n
            grad = dkv[h]
            back = dot_nt(grad, weight_block(h, r))
            block = dot(normed_t[r], grad).astype(BF16)
            tref(h)[j, n, 0, 0:PART, :] = block[0:PART]
            tref(h)[j, n, 1, 0:PART, :] = block[PART:]
            if h:
                back = back + ngrad[:, columns_of(r)]
            if last:
                unit = unit_piece(r)
                gain = jnp.sum(unit * back, axis=0, keepdims=True)
                for part in range(2):
                    t_last[j, n, part, PART:BLOCK, :] = jnp.broadcast_to(gain, (16, SHARE)).astype(
                        BF16
                    )
                back = back * gain_piece(r)
                mean = mean + jnp.sum(back * unit, axis=-1, keepdims=True)
            ngrad[:, columns_of(r)] = back
            return mean

        def group(j, mean):
            mean = lax.fori_loop(0, 4, lambda n, inner: one(j, n, inner), mean)
            pair_copy(h, j).start()
            return mean

        return lax.fori_loop(0, 4, group, jnp.zeros((ROWS, 1), F32))

    token = lax.broadcasted_iota(jnp.int32, (WIDTH, 1), 0) % SPAN
    q_pos = (low_span * SPAN + token, high_span * SPAN + token)

    def load_head(h):
        for n in range(GROUP):
            column = pl.ds(pl.multiple_of((h * GROUP + n) * HEAD, HEAD), HEAD)
            for source, target in ((q_ref, qs), (g_ref, gs)):
                first, second = source[0:SPAN, column], source[SPAN:ROWS, column]
                target[0, n * SPAN : (n + 1) * SPAN, :] = jnp.where(flip, second, first)
                target[1, n * SPAN : (n + 1) * SPAN, :] = jnp.where(flip, first, second)

    def store_head(h):
        for n in range(GROUP):
            column = pl.ds(pl.multiple_of((h * GROUP + n) * HEAD, HEAD), HEAD)
            for source, target in ((qs, q_ref), (gs, g_ref)):
                low = source[0, n * SPAN : (n + 1) * SPAN, :]
                high = source[1, n * SPAN : (n + 1) * SPAN, :]
                target[0:SPAN, column] = jnp.where(flip, high, low)
                target[SPAN:ROWS, column] = jnp.where(flip, low, high)

    def attend(h, half):
        def block(kind, side):
            return kvbuf[h, kind, :, :, side].reshape(RANKS * SPAN, HEAD)

        place_rows = slice(half * WIDTH, (half + 1) * WIDTH)
        q, g = qs[half], gs[half]
        scores = [dot_nt(q, block(0, k)) for k in range(half + 1)]
        scores[half] = jnp.where(
            kpos_ref[half : half + 1, :] <= q_pos[half], scores[half], NEG_FILL
        )
        top = jnp.max(scores[0], axis=-1, keepdims=True)
        if half:
            top = jnp.maximum(top, jnp.max(scores[1], axis=-1, keepdims=True))
        weights = [jnp.exp2((s - top) * EXP_SCALE) for s in scores]
        total = jnp.sum(weights[0], axis=-1, keepdims=True)
        if half:
            total = total + jnp.sum(weights[1], axis=-1, keepdims=True)
        low = [w.astype(BF16) for w in weights]
        attended = dot(low[0], block(1, 0))
        if half:
            attended = attended + dot(low[1], block(1, 1))
        share = 1.0 / total
        attended = (attended * share).astype(BF16)
        grad = (g.astype(F32) * (share * SCALE)).astype(BF16)
        grad_f = grad.astype(F32)
        row_dot = jnp.sum(grad_f * attended.astype(F32), axis=-1, keepdims=True)
        gt[:, place_rows] = jnp.transpose(grad_f).astype(BF16)
        qt[:, place_rows] = jnp.transpose(q.astype(F32)).astype(BF16)
        back = None
        for k in range(half + 1):
            dots = dot_nt(grad, block(1, k))
            ds = (low[k].astype(F32) * (dots - row_dot)).astype(BF16)
            if k:
                probs_high[...] = low[k]
                ds_high[...] = ds
            else:
                probs_low[place_rows, :] = low[k]
                ds_low[place_rows, :] = ds
            term = dot(ds, block(0, k))
            back = term if back is None else back + term
        qs[half] = back.astype(BF16)
        gs[half] = attended

    def key_terms(h):
        for kind, left, low, high in ((0, qt, ds_low, ds_high), (1, gt, probs_low, probs_high)):
            for side, array in (
                (0, dot(left[...], low[...])),
                (1, dot(left[:, WIDTH:], high[...])),
            ):
                grads[h, kind, :, :, side] = (
                    jnp.transpose(array).astype(BF16).reshape(4, 4, SPAN, HEAD)
                )

    w_stage(0, 0)
    w_stage(1, 0)
    late_stage(0)
    loads[0].wait()
    normalise()
    w_stage(0, 1)
    w_stage(1, 1)
    late_stage(1)
    w_stage(0, 2)
    for kind in range(2):
        for db in range(4):
            hand_column(1 - me.core, kind, db).wait_recv()
    project(0)
    kv_stage(0, 0)
    w_stage(1, 2)
    turn()
    kv_stage(0, 1)
    hand_head(1 - me.core, 1).wait_recv()
    project(1)
    kv_stage(1, 0)
    late_stage(2)
    wx[2].stage(0)
    wx[3].stage(0)
    loads[1].wait()
    loads[2].wait()
    kv_stage(0, 2)

    def late_projection(h):
        hand_head(1 - me.core, h).wait_recv()
        project(h)
        kv_stage(h, 0)

    def late_arrival(h):
        wx[h].stage(1)
        hand_head(me.core, h).start()

    def xr_begin(h):
        pair_sum(h)
        xr_stage(h, 0)

    def xr_end(h):
        xr_stage(h, 1)
        ws_stage(h, 0)

    def weights_left():
        for routes in w_routes + [late_routes]:
            for route in routes:
                route.drain()
        for route in wx.values():
            route.drain()
        for kind in range(2):
            for db in range(4):
                hand_column(me.core, kind, db).wait_send()
        for h in range(1, HEADS):
            hand_head(me.core, h).wait_send()

    plan = {
        (0, 0): [lambda: kv_stage(1, 1)],
        (0, 2): [lambda: late_arrival(2), lambda: kv_stage(1, 2)],
        (0, 3): [lambda: rs_stage(0, 0)],
        (0, 4): [lambda: late_projection(2)],
        (1, 1): [lambda: kv_stage(2, 1), lambda: rs_stage(0, 1)],
        (1, 2): [lambda: late_arrival(3), lambda: rs_stage(0, 2), lambda: kv_stage(2, 2)],
        (1, 3): [lambda: rs_stage(1, 0)],
        (1, 4): [lambda: late_projection(3), weights_left, lambda: weight_terms(0)],
        (2, 0): [lambda: kv_stage(3, 1)],
        (2, 1): [lambda: rs_stage(1, 1), lambda: xr_begin(0)],
        (2, 2): [lambda: kv_stage(3, 2), lambda: rs_stage(1, 2)],
        (2, 3): [lambda: rs_stage(2, 0)],
        (2, 4): [lambda: weight_terms(1)],
        (3, 1): [lambda: rs_stage(2, 1), lambda: xr_end(0), lambda: xr_begin(1)],
        (3, 2): [lambda: rs_stage(2, 2), lambda: ws_stage(0, 1)],
        (3, 3): [lambda: rs_stage(3, 0)],
        (3, 4): [lambda: weight_terms(2), lambda: ws_stage(0, 2), lambda: xr_end(1)],
    }

    def one_head(h, carry):
        def serve(point):
            for head in range(HEADS):
                if (head, point) not in plan:
                    continue

                @pl.when(h == head)
                def _():
                    for item in plan[head, point]:
                        item()

        load_head(h)
        serve(0)
        attend(h, 0)
        serve(1)
        attend(h, 1)
        serve(2)
        key_terms(h)
        serve(3)
        store_head(h)
        serve(4)
        return carry

    lax.fori_loop(0, HEADS, one_head, 0)

    stores = [
        pltpu.make_async_copy(g_ref, out_hbm, io_sem.at[0]),
        pltpu.make_async_copy(q_ref, dq_hbm, io_sem.at[1]),
    ]
    for copy in stores:
        copy.start()

    def x_copy(index, ref, dst, to):
        return pltpu.make_async_remote_copy(
            src_ref=ref,
            dst_ref=dst,
            send_sem=x_ssem.at[index],
            recv_sem=x_rsem.at[index],
            device_id=to,
            device_id_type=MESH,
        )

    def spread(base, heads, d, owner):
        ref = final.at[me.core, heads, piece_rows(owner)]
        return x_copy(base + d - 1, ref, ref, me.along_x(d))

    def to_partner(index, heads, core):
        ref = final.at[core, heads]
        return x_copy(index, ref, ref, me.partner())

    def spread_start(base, heads):
        for d in (1, 2, 3):
            spread(base, heads, d, me.x).start()

    def spread_wait(base, heads):
        for d in (1, 2, 3):
            spread(base, heads, d, (me.x + 4 - d) % 4).wait_recv()

    early_heads, late_head = pl.ds(0, HEADS - 1), pl.ds(HEADS - 1, 1)
    rs_stage(3, 1)
    xr_begin(2)
    ws_stage(1, 1)
    rs_stage(3, 2)
    mean = weight_terms(3) * (1.0 / FEATURES)
    pair_sum(3)
    ws_stage(3, 0)
    ws_stage(1, 2)
    xr_end(2)

    def row_grad(r, carry):
        dx = inv_ref[...] * (ngrad[:, columns_of(r)] - unit_piece(r) * mean)
        x_ref[:, columns_of(r)] = dx.astype(BF16)
        return carry

    lax.fori_loop(0, RANKS, row_grad, 0)
    stores.append(pltpu.make_async_copy(x_ref, dx_hbm, io_sem.at[2]))
    stores[2].start()
    ws_stage(3, 1)
    ws_stage(2, 1)
    ws_stage(3, 2)
    xr_stage(3, 0)
    gains = [
        x_copy(5 + d, x_send.at[pl.ds(PART, 16)], x_gain.at[d - 1], me.along_x(d))
        for d in (1, 2, 3)
    ]
    for copy in gains:
        copy.start()
    ws_stage(2, 2)
    spread_start(0, early_heads)
    xr_stage(3, 1)
    final[me.core, HEADS - 1, piece_rows(me.x)] = x_send[piece_rows(me.x), :]
    spread_start(3, late_head)
    spread_wait(0, early_heads)
    to_partner(9, early_heads, me.core).start()
    for copy in gains:
        copy.wait_recv()
    total = x_send[PART:BLOCK, :].astype(F32)
    for d in range(3):
        total = total + x_gain[d].astype(F32)
    dgain_ref[...] = total[0:8, :]
    spread_wait(3, late_head)
    to_partner(10, late_head, me.core).start()

    def write_weights(heads):
        for h in heads:
            for core in range(2):
                rows, columns = slice(core * PART, (core + 1) * PART), slice(h * HEAD, (h + 1) * HEAD)
                dwk_ref[rows, columns] = final[core, h, :, 0:HEAD].astype(F32)
                dwv_ref[rows, columns] = final[core, h, :, HEAD:].astype(F32)

    to_partner(9, early_heads, 1 - me.core).wait_recv()
    write_weights(range(HEADS - 1))
    to_partner(10, late_head, 1 - me.core).wait_recv()
    write_weights((HEADS - 1,))

    for routes in kv_routes + rs_routes + ws_routes:
        for route in routes:
            route.drain()
    for route in xr_routes:
        route.drain()
    for h in range(HEADS):
        for j in range(4):
            pair_copy(h, j).wait_send()
    for copy in gains:
        copy.wait_send()
    for base, heads in ((0, early_heads), (3, late_head)):
        for d in (1, 2, 3):
            spread(base, heads, d, me.x).wait_send()
    to_partner(9, early_heads, me.core).wait_send()
    to_partner(10, late_head, me.core).wait_send()
    for copy in stores:
        copy.wait()


def settle(*refs):
    count = len(refs) // 2
    for n in range(count):
        refs[count + n][...] = refs[n][...]


def local(inputs, queries, out_grad, span_ids, norm_gain, key_weight, value_weight):
    rank = lax.axis_index("shard") * 8 + lax.axis_index("ctx")
    spans = span_ids.reshape(RANKS, 2)
    own = lax.dynamic_slice_in_dim(spans, rank, 1, 0).reshape(2, 1)
    token = jnp.arange(SPAN, dtype=jnp.int32)[None, :]
    own_pos = (own * SPAN + token).reshape(ROWS)
    ordered = spans.reshape(2, 2, 4, 2).transpose(1, 0, 2, 3).reshape(RANKS, 2)
    low = jnp.minimum(ordered[:, 0], ordered[:, 1])[:, None] * SPAN + token
    high = jnp.maximum(ordered[:, 0], ordered[:, 1])[:, None] * SPAN + token
    kpos = jnp.stack([low.reshape(-1), high.reshape(-1)])
    half = HEAD // 2
    frequency = jnp.exp(
        -math.log(ROPE_BASE) * (2.0 * jnp.arange(half, dtype=jnp.float32) / HEAD)
    )
    angles = own_pos.astype(jnp.float32)[:, None] * frequency[None, :]
    cosine, sine = jnp.cos(angles), jnp.sin(angles)
    cosine = jnp.concatenate([cosine, cosine], axis=1)
    sine = jnp.concatenate([-sine, sine], axis=1)

    vmem = pl.BlockSpec(memory_space=pltpu.VMEM)
    smem = pl.BlockSpec(memory_space=pltpu.SMEM)
    anywhere = pl.BlockSpec(memory_space=pl.ANY)
    dma = pltpu.SemaphoreType.DMA
    outs = pl.pallas_call(
        kernel,
        out_shape=[
            jax.ShapeDtypeStruct((ROWS, FEATURES), BF16),
            jax.ShapeDtypeStruct((ROWS, FEATURES), BF16),
            jax.ShapeDtypeStruct((ROWS, FEATURES), BF16),
            jax.ShapeDtypeStruct((SHARE, WIDTH), F32),
            jax.ShapeDtypeStruct((SHARE, WIDTH), F32),
            jax.ShapeDtypeStruct((8, SHARE), F32),
        ],
        in_specs=[anywhere] * 3 + [smem] + [vmem] * 6,
        out_specs=[anywhere] * 3 + [vmem] * 3,
        scratch_shapes=[
            pltpu.VMEM((ROWS, FEATURES), BF16),
            pltpu.VMEM((ROWS, FEATURES), BF16),
            pltpu.VMEM((ROWS, FEATURES), BF16),
            pltpu.VMEM((4, 4, 2, BLOCK, 2 * HEAD), BF16),
            pltpu.VMEM((HEADS - 1, 4, 4, 2, PART, 2 * HEAD), BF16),
            pltpu.VMEM((HEADS, 2, 4, 4, 2, SPAN, HEAD), BF16),
            pltpu.VMEM((2, WIDTH, HEAD), BF16),
            pltpu.VMEM((2, WIDTH, HEAD), BF16),
            pltpu.VMEM((HEAD, 2 * WIDTH), BF16),
            pltpu.VMEM((HEAD, 2 * WIDTH), BF16),
            pltpu.VMEM((2 * WIDTH, RANKS * SPAN), BF16),
            pltpu.VMEM((WIDTH, RANKS * SPAN), BF16),
            pltpu.VMEM((2 * WIDTH, RANKS * SPAN), BF16),
            pltpu.VMEM((WIDTH, RANKS * SPAN), BF16),
            pltpu.VMEM((HEADS, 2, 4, 4, 2, SPAN, HEAD), BF16),
            pltpu.VMEM((HEADS, 2, 3, 4, 2, SPAN, HEAD), BF16),
            pltpu.VMEM((HEADS, 2, 3, 2, SPAN, HEAD), BF16),
            pltpu.VMEM((HEADS, ROWS, 2 * HEAD), BF16),
            pltpu.VMEM((ROWS, FEATURES), F32),
            pltpu.VMEM((RANKS, SHARE, ROWS), BF16),
            pltpu.VMEM((4, 4, 2, BLOCK, 2 * HEAD), BF16),
            pltpu.VMEM((4, 4, BLOCK, 2 * HEAD), BF16),
            pltpu.VMEM((HEADS - 1, 4, 4, PART, 2 * HEAD), BF16),
            pltpu.VMEM((HEADS - 1, 2, 3, 4, 32, HEAD), BF16),
            pltpu.VMEM((HEADS - 1, 2, 3, 32, HEAD), BF16),
            pltpu.VMEM((2, 3, 4, 80, 2 * HEAD), BF16),
            pltpu.VMEM((2, 3, 80, 2 * HEAD), BF16),
            pltpu.VMEM((HEADS - 1, 3, 4, 4, 32, 2 * HEAD), BF16),
            pltpu.VMEM((3, 32, 2 * HEAD), BF16),
            pltpu.VMEM((BLOCK, 2 * HEAD), BF16),
            pltpu.VMEM((3, 16, 2 * HEAD), BF16),
            pltpu.VMEM((2, HEADS, PART, 2 * HEAD), BF16),
            pltpu.VMEM((ROWS, 1), F32),
            dma((3,)),
            dma((EARLY + 1, 2, 6)), dma((EARLY + 1, 2, 6)),
            dma((7 + HEADS,)), dma((7 + HEADS,)),
            dma((HEADS - EARLY, 3)), dma((HEADS - EARLY, 3)),
            dma((HEADS, 2, 6)), dma((HEADS, 2, 6)),
            dma((HEADS, 2, 6)), dma((HEADS, 2, 6)),
            dma((HEADS, 4)), dma((HEADS, 4)),
            dma((HEADS, 2, 6)), dma((HEADS, 2, 6)),
            dma((HEADS, 3)), dma((HEADS, 3)),
            dma((11,)), dma((11,)),
        ],
        compiler_params=pltpu.CompilerParams(
            collective_id=0, has_side_effects=True, vmem_limit_bytes=55 * 1024 * 1024
        ),
        cost_estimate=pl.CostEstimate(
            flops=12 * 10**9, bytes_accessed=10**7, transcendentals=7 * 10**6
        ),
        name="layer",
    )(
        inputs, queries, out_grad, spans.reshape(-1), kpos, norm_gain.reshape(1, SHARE),
        key_weight, value_weight, cosine, sine,
    )
    blocks = [pl.BlockSpec((ROWS, FEATURES // 4), lambda i: (0, i))] * 3
    blocks += [pl.BlockSpec((SHARE // 4, WIDTH), lambda i: (i, 0))] * 2
    blocks += [pl.BlockSpec((8, SHARE), lambda i: (0, 0))]
    outs = pl.pallas_call(
        settle,
        out_shape=[jax.ShapeDtypeStruct(o.shape, o.dtype) for o in outs],
        grid=(4,),
        in_specs=blocks,
        out_specs=blocks,
        name="settle",
    )(*outs)
    return (*outs[:5], outs[5][0])


def solution(mesh):
    tokens = P(("dp", "shard", "ctx"), None)
    rows = P(("shard", "ctx"), None)
    return jax.shard_map(
        local,
        mesh=mesh,
        in_specs=(tokens, tokens, tokens, P("dp", None, None), P(("shard", "ctx")), rows, rows),
        out_specs=(tokens, tokens, tokens, rows, rows, P(("shard", "ctx"))),
        check_vma=False,
    )
```

time: 847 us -> 167 us (0.20)
  waiting for transfers between devices: 466 us -> 0 us
  Pallas kernels: 0 us -> 159 us
  blocking collectives: 129 us -> 0 us
  matrix products: 95.4 us -> 0 us
  local copies, waits for them, and re-layouts: 88.5 us -> 4.24 us
  other arithmetic: 40 us -> 2.02 us
  between operations: 15.2 us -> 0.67 us
    reduce_scatter x3 -> x0, waiting for transfers between devices: 202 us -> none  [the longest x1 106 us: local(): lax.psum_scatter(kv_acc, ('shard', 'ctx'), scatter_dimension=0, tiled=True)]
    all_gather x3 -> x0, waiting for transfers between devices: 197 us -> none  [the longest x1 80.3 us: local(): lax.all_gather(value_weight, ('shard', 'ctx'), axis=0, tiled=True)]
    pallas_call x0 -> x2, Pallas kernels: none -> 159 us  [the longest x1 155 us: local(): pl.pallas_call(kernel, out_shape=[jax.ShapeDtypeStruct((ROWS, FEATURES),...]
    dot_general x34 -> x0, matrix products: 95.4 us -> none  [the longest x4 17.7 us: backward_step(): jnp.einsum('tkgd,nkd->kgtn', grouped_g, value_part, preferred_element_typ...]
    unnamed x1 -> x0, blocking collectives: 65.8 us -> none
    psum x1 -> x0, waiting for transfers between devices: 65.5 us -> none  [local(): lax.psum((key_share, value_share, gain_share), 'dp')]
    dynamic_update_slice x4 -> x0, local copies, waits for them, and re-layouts: 41.1 us -> none  [backward_step(): kv_acc = lax.dynamic_update_slice_in_dim(kv_acc, current + update, start, 0)]
    all_gather x1 -> x0, blocking collectives: 35.5 us -> none  [local(): lax.all_gather(norm_gain, ('shard', 'ctx'), axis=0, tiled=True)]
  transfers between devices with their start and end apart: 7 -> 0, of which waited for: 6 -> 0; matrix products, arithmetic and copies ran while one was open for 3% -> 0% of each run, Pallas kernels for 0% -> 0%
where the time goes in v2:
time: 167 us; the launch traced here: 166 us
  Pallas kernels  159 us (95%)
  local copies, waits for them, and re-layouts  4.24 us (3%)
  other arithmetic  2.02 us (1%)
    pallas_call x1, Pallas kernels, local(): pl.pallas_call(kernel, out_shape=[jax.ShapeDtypeStruct((ROWS, FEATURES),...  155 us
    pallas_call x1, Pallas kernels, local(): pl.pallas_call(settle, out_shape=[jax.ShapeDtypeStruct(o.shape, o.dtype)...  4.8 us

profile of v2, /device:TPU:1, one launch (start us, length us, event | category | flops | bytes accessed | tf_op | source)
XLA Modules:
  0.0 166.4 jit_solution(11770618862380695242)
XLA Ops:
  0.6 0.0 copy-start
  0.6 0.7 copy-done
  1.3 0.2 multiply_reduce_fusion
  1.5 0.1 add_convert_fusion
  1.6 0.1 convert_element_type.11
  1.7 0.0 copy-start.1
  1.7 0.6 copy-done.1
  2.3 0.6 reshape.98.gain_ref
  2.9 0.1 reshape_reshape.7
  3.0 0.1 reshape.97
  3.1 0.1 copy.15
  3.2 0.6 reshape_reshape.6.spans_ref
  3.8 0.1 iota_add_fusion
  3.8 0.1 add.84
  3.9 0.1 add.79
  4.0 0.6 pad_add_fusion.kpos_ref
  4.6 0.3 fusion
  4.9 0.8 pad_maximum_fusion
  5.7 154.7 %layer.1 = (bf16[128,4096]{1,0:T(8,128)(2,1)}, bf16[128,4096]{1,0:T(8,128)(2,1)}, bf16[128,4096]{1,0:T(8,128)(2,1)}, f32[256,512]{1,0:T(8,128)}, f32[256,512]{1,0:T(8,128)}, /*index=5*/f32[8,256]{1,0:T(8,128)}) custom-call(bf16[128,4096]{1,0:T(8,128)(2,1)} %x_hbm.1, bf16[128,4096]{1,0:T(8,128)(2,1)} %q_hbm.1, bf16[128,4096]{1,0:T(8,128)(2,1)} %g_hbm.1, ...), custom_call_target="tpu_custom_call" | custom-call | flops 12000000000 | bytes 10000000 | tf_op jit(solution)/shard_map/layer/pallas_call | solution.py:875
  160.4 4.8 %settle.1 = (bf16[128,4096]{1,0:T(8,128)(2,1)}, bf16[128,4096]{1,0:T(8,128)(2,1)}, bf16[128,4096]{1,0:T(8,128)(2,1)}, f32[256,512]{1,0:T(8,128)}, f32[256,512]{1,0:T(8,128)}, /*index=5*/f32[8,256]{1,0:T(8,128)}) custom-call(bf16[128,4096]{1,0:T(8,128)(2,1)} %get-tuple-element.18.refs_0_, bf16[128,4096]{1,0:T(8,128)(2,1)} %get-tuple-element.19.refs_1_, ...), custom_call_target="tpu_custom_call" | custom-call | tf_op jit(solution)/shard_map/settle/pallas_call | solution.py:946
  165.2 1.3 slice.13
  (3 shorter events, 0.0 us)
Async XLA Ops:
  0.6 0.7 copy-start
  1.7 0.7 copy-start.1

commit v3 on v2

--- a/solution.py
+++ b/solution.py
@@ -3,6 +3,7 @@
 
 import jax
 import jax.numpy as jnp
+import numpy as np
 from jax import lax
 from jax.experimental import pallas as pl
 from jax.experimental.pallas import tpu as pltpu
@@ -18,8 +19,9 @@
 SHARE = 256
 WIDTH = 512
 BLOCK = 144
+FOUR = 1024
 PART = 128
-EARLY = 2
+EARLY = 1
 EPSILON = 1e-05
 ROPE_BASE = 500000.0
 NEG_FILL = -1e30
@@ -81,8 +83,8 @@
 
 
 class Route:
-    def __init__(self, place, kind, slot, send, recv):
-        self.place, self.kind, self.slot = place, kind, slot
+    def __init__(self, place, kind, slot, half, send, recv):
+        self.place, self.kind, self.slot, self.half = place, kind, slot, half
         self.send_sems, self.recv_sems = send, recv
         self.a, self.b = (place.z, place.y) if kind else (place.y, place.z)
 
@@ -110,59 +112,75 @@
         )
 
     def drain(self):
-        for n in range(6):
+        for n in range(7):
             self.message(n).wait_send()
 
 
 class Gather(Route):
     def message(self, n, back=False):
-        step = STEPS[n % 3]
         if n < 3:
-            ref = self.block(4 - step if back else 0, 0)
-            return self.copy(n, ref, ref, self.device(step, 0))
-        ref = self.column(4 - step if back else 0)
+            ref = self.block(4 - STEPS[n] if back else 0, 0)
+            return self.copy(n, ref, ref, self.device(STEPS[n], 0))
+        step = 1 if n % 2 else 3
+        if n < 5:
+            ref = self.column(4 - step if back else 0)
+        else:
+            ref = self.half(self.column(2 if back else 4 - step), n - 5)
         return self.copy(n, ref, ref, self.device(0, step))
 
-    def stage(self, number, arrived=None):
+    def stage(self, number, arrived=lambda db: None):
         if number == 0:
             start_all([self.message(n) for n in range(3)])
         elif number == 1:
             for n in range(3):
                 self.message(n, True).wait_recv()
-            start_all([self.message(n) for n in range(3, 6)])
-            if arrived is not None:
-                arrived(0)
+            start_all([self.message(n) for n in (3, 4)])
+            arrived(0)
+        elif number == 2:
+            for n, db in ((3, 3), (4, 1)):
+                self.message(n, True).wait_recv()
+                self.message(n + 2).start()
+                arrived(db)
         else:
-            for n in range(3, 6):
+            for n in (5, 6):
                 self.message(n, True).wait_recv()
-                if arrived is not None:
-                    arrived(4 - STEPS[n - 3])
+            arrived(2)
 
 
 class Scatter(Route):
-    def __init__(self, place, kind, slot, columns, blocks, send, recv):
-        super().__init__(place, kind, slot, send, recv)
-        self.columns, self.blocks = columns, blocks
+    def __init__(self, place, kind, slot, half, halves, columns, blocks, send, recv):
+        super().__init__(place, kind, slot, half, send, recv)
+        self.halves, self.columns, self.blocks = halves, columns, blocks
 
     def message(self, n):
-        step = STEPS[n % 3]
-        if n < 3:
-            return self.copy(n, self.column(step), self.columns(n), self.device(0, step))
-        return self.copy(n, self.block(step, 0), self.blocks(n - 3), self.device(step, 0))
+        if n < 4:
+            step = 3 if n % 2 else 1
+            if n < 2:
+                src, dst = self.half(self.column(2), n), self.halves(n)
+            else:
+                src, dst = self.column(step), self.columns(n - 2)
+            return self.copy(n, src, dst, self.device(0, step))
+        step = STEPS[n - 4]
+        return self.copy(n, self.block(step, 0), self.blocks(n - 4), self.device(step, 0))
 
     def stage(self, number):
         if number == 0:
-            start_all([self.message(n) for n in range(3)])
+            start_all([self.message(n) for n in range(2)])
         elif number == 1:
-            for n in range(3):
+            for n, step in ((0, 1), (1, 3)):
+                self.message(n).wait_recv()
+                add_into(self.half(self.column(step), n), [self.halves(n)])
+                self.message(n + 2).start()
+        elif number == 2:
+            for n in (2, 3):
                 self.message(n).wait_recv()
             for n, step in enumerate(STEPS + (0,)):
                 place = (self.a + step) % 4
-                add_into(self.block(step, 0), [self.columns(i).at[place] for i in range(3)])
+                add_into(self.block(step, 0), [self.columns(i).at[place] for i in range(2)])
                 if step:
-                    self.message(3 + n).start()
+                    self.message(4 + n).start()
         else:
-            for n in range(3, 6):
+            for n in range(4, 7):
                 self.message(n).wait_recv()
 
     def total(self):
@@ -215,16 +233,22 @@
     return pl.ds(64, 80 if with_gain else 64) if kind else pl.ds(0, 64)
 
 
+def tall_half(ref, kind, with_gain, n):
+    if n == 0:
+        return ref.at[:, pl.ds(0, 32)]
+    return ref.at[:, pl.ds(32, 48 if kind and with_gain else 32)]
+
+
 def piece_rows(number):
     return pl.ds(pl.multiple_of(number * 32, 32), 32)
 
 
 def kernel(
-    x_hbm, q_hbm, g_hbm, spans_ref, kpos_ref, gain_ref, wk_ref, wv_ref, cos_ref, sin_ref,
+    x_hbm, q_hbm, g_hbm, spans_ref, gain_ref, wk_hbm, wv_hbm, frequency_ref,
     out_hbm, dq_hbm, dx_hbm, dwk_ref, dwv_ref, dgain_ref,
     x_ref, q_ref, g_ref, w_first, w_rest, kvbuf, qs, gs, qt, gt, probs_low, probs_high, ds_low, ds_high,
-    grads, kv_columns, kv_blocks, dkv, ngrad, normed_t, t_last, p_last, p_rest, q_columns, q_blocks,
-    w_columns, w_blocks, r_land, l_land, x_send, x_gain, final, inv_ref,
+    grads, kv_halves, kv_columns, kv_blocks, dkv, ngrad, normed, normed_t, gain_row, t_last, p_last, p_rest, q_halves, q_columns, q_blocks,
+    w_halves, w_columns, w_blocks, r_land, l_land, x_send, x_gain, final, inv_ref, kpos_ref, cos_ref, sin_ref,
     io_sem, w_send, w_recv, hand_send, hand_recv, wx_send, wx_recv, kv_send, kv_recv,
     rs_send, rs_recv, pair_send, pair_recv, ws_send, ws_recv, xr_send, xr_recv, x_ssem, x_rsem,
 ):
@@ -247,20 +271,36 @@
     for copy in loads:
         copy.start()
 
-    for h in range(HEADS):
-        columns = slice(h * HEAD, (h + 1) * HEAD)
-        for part in range(2):
-            rows = slice(part * PART, (part + 1) * PART)
-            wref(h)[me.z, me.y, part, 0:PART, 0:HEAD] = wk_ref[rows, columns]
-            wref(h)[me.z, me.y, part, 0:PART, HEAD : 2 * HEAD] = wv_ref[rows, columns]
-    for part in range(2):
-        w_first[me.z, me.y, part, PART:BLOCK, :] = jnp.broadcast_to(gain_ref[...], (16, SHARE))
-
     others = [device_at(me.x, me.core, (me.y + d) % 4, me.z) for d in (1, 2, 3)]
     others += [device_at(me.x, me.core, me.y, (me.z + d) % 4) for d in (1, 2, 3)]
     others += [me.along_x(d) for d in (1, 2, 3)] + [me.partner()]
     for other in others:
         pl.semaphore_signal(barrier, inc=1, device_id=other, device_id_type=MESH)
+
+    def own_weights(h, n, source):
+        if h < EARLY:
+            rows, target = pl.ds(pl.multiple_of(me.core * PART, PART), PART), pl.ds(0, PART)
+        else:
+            rows = pl.ds(pl.multiple_of(me.core * PART + me.x * 32, 32), 32)
+            target = piece_rows(me.x)
+        return pltpu.make_async_copy(
+            source.at[rows, pl.ds(h * HEAD, HEAD)],
+            wref(h).at[me.z, me.y, me.core, target, pl.ds(n * HEAD, HEAD)],
+            io_sem.at[3 + 2 * h + n],
+        )
+
+    own = [
+        own_weights(h, n, source)
+        for h in range(HEADS)
+        for n, source in enumerate((wk_hbm, wv_hbm))
+    ]
+    for copy in own:
+        copy.start()
+    w_first[me.z, me.y, me.core, PART:BLOCK, :] = jnp.broadcast_to(
+        gain_ref[...].reshape(1, SHARE), (16, SHARE)
+    )
+    for copy in own:
+        copy.wait()
     pl.semaphore_wait(barrier, len(others))
 
     w_routes = [
@@ -269,6 +309,7 @@
                 me,
                 kind,
                 lambda z, y, h=h, kind=kind: wref(h).at[z, y, me.core, tall_rows(kind, h == 0)],
+                lambda ref, n, kind=kind: tall_half(ref, kind, True, n),
                 w_send.at[h, kind],
                 w_recv.at[h, kind],
             )
@@ -284,6 +325,7 @@
             lambda z, y, kind=kind: w_rest.at[
                 pl.ds(EARLY - 1, HEADS - EARLY), z, y, me.core, piece_rows(me.x), pl.ds(kind * HEAD, HEAD)
             ],
+            lambda ref, n: ref.at[:, :, pl.ds(16 * n, 16)],
             w_send.at[EARLY, kind],
             w_recv.at[EARLY, kind],
         )
@@ -325,12 +367,7 @@
 
     def w_stage(h, number):
         for kind, route in enumerate(w_routes[h]):
-            if h:
-                route.stage(number)
-            else:
-                route.stage(number, lambda db, kind=kind: hand_column(me.core, kind, db).start())
-        if h and number == 2:
-            hand_head(me.core, h).start()
+            route.stage(number, lambda db, kind=kind: hand_column(me.core, kind, db).start())
 
     def late_stage(number):
         for route in late_routes:
@@ -342,6 +379,7 @@
                 me,
                 kind,
                 lambda z, y, h=h, kind=kind: kvbuf.at[h, kind, z, y],
+                lambda ref, n: ref.at[:, n],
                 kv_send.at[h, kind],
                 kv_recv.at[h, kind],
             )
@@ -360,6 +398,8 @@
                 me,
                 kind,
                 lambda z, y, h=h, kind=kind: grads.at[h, kind, z, y],
+                lambda ref, n: ref.at[:, n],
+                lambda n, h=h, kind=kind: kv_halves.at[h, kind, n],
                 lambda n, h=h, kind=kind: kv_columns.at[h, kind, n],
                 lambda n, h=h, kind=kind: kv_blocks.at[h, kind, n],
                 rs_send.at[h, kind],
@@ -370,8 +410,8 @@
         for h in range(HEADS)
     ]
 
-    first_span = spans_ref[2 * me.rank]
-    second_span = spans_ref[2 * me.rank + 1]
+    first_span = spans_ref[0, me.rank, 0]
+    second_span = spans_ref[0, me.rank, 1]
     flip = first_span > second_span
     low_span = jnp.minimum(first_span, second_span)
     high_span = jnp.maximum(first_span, second_span)
@@ -379,7 +419,7 @@
     def rs_stage(h, number):
         for kind, route in enumerate(rs_routes[h]):
             route.stage(number)
-            if number < 2:
+            if number < 3:
                 continue
             total = route.total()
             low, high = total[0], total[1]
@@ -409,11 +449,7 @@
         def group(j, carry):
             pair_copy(h, j).wait_recv()
 
-            def one(n, inner):
-                add_into(tref(h).at[j, n, me.core, term_rows(h)], [pref(h).at[j, n]])
-                return inner
-
-            lax.fori_loop(0, 4, one, 0)
+            add_into(tref(h).at[j, :, me.core, term_rows(h)], [pref(h).at[j]])
             return carry
 
         lax.fori_loop(0, 4, group, 0)
@@ -445,6 +481,8 @@
                 lambda z, y, h=h, kind=kind: tref(h).at[
                     z, y, me.core, piece_rows(me.x), pl.ds(kind * HEAD, HEAD)
                 ],
+                lambda ref, n: ref.at[:, pl.ds(16 * n, 16)],
+                lambda n, h=h, kind=kind: q_halves.at[h, kind, n],
                 lambda n, h=h, kind=kind: q_columns.at[h, kind, n],
                 lambda n, h=h, kind=kind: q_blocks.at[h, kind, n],
                 ws_send.at[h, kind],
@@ -460,6 +498,8 @@
                 me,
                 kind,
                 lambda z, y, kind=kind: t_last.at[z, y, me.core, tall_rows(kind, True)],
+                lambda ref, n, kind=kind: tall_half(ref, kind, True, n),
+                lambda n, kind=kind: w_halves.at[kind, n, :, pl.ds(0, 48 if kind and n else 32)],
                 lambda n, kind=kind: w_columns.at[kind, n, :, pl.ds(0, 80 if kind else 64)],
                 lambda n, kind=kind: w_blocks.at[kind, n, pl.ds(0, 80 if kind else 64)],
                 ws_send.at[HEADS - 1, kind],
@@ -475,7 +515,7 @@
     def ws_stage(h, number):
         for kind, route in enumerate(ws_routes[h]):
             route.stage(number)
-            if number < 2:
+            if number < 3:
                 continue
             total = route.total().astype(BF16)
             if h < HEADS - 1:
@@ -485,17 +525,32 @@
             else:
                 x_send[64 * kind : 64 * kind + (80 if kind else 64), :] = total
 
-    def columns_of(r):
-        return pl.ds(pl.multiple_of(rank_at(r % 4, r // 4) * SHARE, SHARE), SHARE)
-
-    def unit_piece(r):
-        return x_ref[:, columns_of(r)].astype(F32) * inv_ref[...]
-
-    def gain_piece(r):
-        return w_first[r // 4, r % 4, 0, PART:BLOCK, :].astype(F32)[0:1, :]
-
-    def weight_block(h, r):
-        return wref(h)[r // 4, r % 4, :, 0:PART, :].reshape(SHARE, 2 * HEAD)
+    def columns_of(j):
+        return pl.ds(pl.multiple_of(((j % 2) * 2 + j // 2) * FOUR, FOUR), FOUR)
+
+    def unit_piece(j):
+        return x_ref[:, columns_of(j)].astype(F32) * inv_ref[...]
+
+    def weight_block(h, j):
+        return wref(h)[j, :, :, 0:PART, :].reshape(FOUR, 2 * HEAD)
+
+    def positions():
+        row = lax.broadcasted_iota(jnp.int32, (ROWS, 1), 0)
+        place = jnp.where(row < SPAN, first_span * SPAN + row, second_span * SPAN + row - SPAN)
+        angle = place.astype(F32) * frequency_ref[...]
+        lane = lax.broadcasted_iota(jnp.int32, (ROWS, HEAD), 1)
+        sine = jnp.sin(angle)
+        cos_ref[...] = jnp.cos(angle)
+        sin_ref[...] = jnp.where(lane < HEAD // 2, -sine, sine)
+        lane = lax.broadcasted_iota(jnp.int32, (1, HEAD), 1)
+        for s in range(0, RANKS, 2):
+            ranks = [rank_at((s + n) % 4, (s + n) // 4) for n in range(2)]
+            pairs = [(spans_ref[0, r, 0], spans_ref[0, r, 1]) for r in ranks]
+            for half, pick in ((0, jnp.minimum), (1, jnp.maximum)):
+                left, right = pick(*pairs[0]), pick(*pairs[1])
+                kpos_ref[half : half + 1, s * SPAN : s * SPAN + HEAD] = jnp.where(
+                    lane < SPAN, left * SPAN + lane, right * SPAN + lane - SPAN
+                )
 
     def normalise():
         squares = jnp.zeros((ROWS, HEAD), F32)
@@ -506,23 +561,22 @@
             jnp.sum(squares, axis=-1, keepdims=True) * (1.0 / FEATURES) + EPSILON
         )
 
-    def normed_piece(r):
-        return unit_piece(r) * gain_piece(r)
+    def prepare():
+        for j in range(4):
+            for y in range(4):
+                gain_row[j, :, y * SHARE : (y + 1) * SHARE] = w_first[
+                    j, y, 0, PART:BLOCK, :
+                ].astype(F32)[0:1, :]
+            normed[j] = (unit_piece(j) * gain_row[j]).astype(BF16)
 
     def turn():
-        def one(r, carry):
-            normed_t[r] = jnp.transpose(normed_piece(r)).astype(BF16)
-            return carry
-
-        lax.fori_loop(0, RANKS, one, 0)
+        for j in range(4):
+            normed_t[j] = jnp.transpose(normed[j].astype(F32)).astype(BF16)
 
     def project(h):
-        raw = lax.fori_loop(
-            0,
-            RANKS,
-            lambda r, total: total + dot(normed_piece(r).astype(BF16), weight_block(h, r)),
-            jnp.zeros((ROWS, 2 * HEAD), F32),
-        )
+        raw = dot(normed[0], weight_block(h, 0))
+        for j in range(1, 4):
+            raw = raw + dot(normed[j], weight_block(h, j))
         key = raw[:, 0:HEAD]
         key = key * cos_ref[...] + pltpu.roll(key, HEAD // 2, 1) * sin_ref[...]
         for kind, array in ((0, key), (1, raw[:, HEAD:])):
@@ -532,29 +586,23 @@
     def weight_terms(h):
         last = h == HEADS - 1
 
-        def one(j, n, mean):
-            r = 4 * j + n
+        def group(j, mean):
             grad = dkv[h]
-            back = dot_nt(grad, weight_block(h, r))
-            block = dot(normed_t[r], grad).astype(BF16)
-            tref(h)[j, n, 0, 0:PART, :] = block[0:PART]
-            tref(h)[j, n, 1, 0:PART, :] = block[PART:]
+            back = dot_nt(grad, weight_block(h, j))
+            block = dot(normed_t[j], grad).astype(BF16)
+            tref(h)[j, :, :, 0:PART, :] = block.reshape(4, 2, PART, 2 * HEAD)
             if h:
-                back = back + ngrad[:, columns_of(r)]
+                back = back + ngrad[j]
             if last:
-                unit = unit_piece(r)
+                unit = unit_piece(j)
                 gain = jnp.sum(unit * back, axis=0, keepdims=True)
-                for part in range(2):
-                    t_last[j, n, part, PART:BLOCK, :] = jnp.broadcast_to(gain, (16, SHARE)).astype(
-                        BF16
-                    )
-                back = back * gain_piece(r)
+                for y in range(4):
+                    piece = jnp.broadcast_to(gain[:, y * SHARE : (y + 1) * SHARE], (16, SHARE))
+                    for part in range(2):
+                        t_last[j, y, part, PART:BLOCK, :] = piece.astype(BF16)
+                back = back * gain_row[j]
                 mean = mean + jnp.sum(back * unit, axis=-1, keepdims=True)
-            ngrad[:, columns_of(r)] = back
-            return mean
-
-        def group(j, mean):
-            mean = lax.fori_loop(0, 4, lambda n, inner: one(j, n, inner), mean)
+            ngrad[j] = back
             pair_copy(h, j).start()
             return mean
 
@@ -633,41 +681,43 @@
                     jnp.transpose(array).astype(BF16).reshape(4, 4, SPAN, HEAD)
                 )
 
-    w_stage(0, 0)
-    w_stage(1, 0)
-    late_stage(0)
-    loads[0].wait()
-    normalise()
-    w_stage(0, 1)
-    w_stage(1, 1)
-    late_stage(1)
-    w_stage(0, 2)
-    for kind in range(2):
-        for db in range(4):
-            hand_column(1 - me.core, kind, db).wait_recv()
-    project(0)
-    kv_stage(0, 0)
-    w_stage(1, 2)
-    turn()
-    kv_stage(0, 1)
-    hand_head(1 - me.core, 1).wait_recv()
-    project(1)
-    kv_stage(1, 0)
-    late_stage(2)
-    wx[2].stage(0)
-    wx[3].stage(0)
-    loads[1].wait()
-    loads[2].wait()
-    kv_stage(0, 2)
+    def late_arrival(h):
+        wx[h].stage(1)
+        hand_head(me.core, h).start()
 
     def late_projection(h):
         hand_head(1 - me.core, h).wait_recv()
         project(h)
         kv_stage(h, 0)
 
-    def late_arrival(h):
-        wx[h].stage(1)
-        hand_head(me.core, h).start()
+    late_stage(0)
+    w_stage(0, 0)
+    positions()
+    loads[0].wait()
+    normalise()
+    late_stage(1)
+    w_stage(0, 1)
+    late_stage(2)
+    w_stage(0, 2)
+    late_stage(3)
+    for h in range(EARLY, HEADS):
+        wx[h].stage(0)
+    w_stage(0, 3)
+    for kind in range(2):
+        for db in range(4):
+            hand_column(1 - me.core, kind, db).wait_recv()
+    prepare()
+    project(0)
+    kv_stage(0, 0)
+    turn()
+    kv_stage(0, 1)
+    late_arrival(1)
+    kv_stage(0, 2)
+    late_projection(1)
+    loads[1].wait()
+    loads[2].wait()
+    load_head(0)
+    kv_stage(0, 3)
 
     def xr_begin(h):
         pair_sum(h)
@@ -690,23 +740,23 @@
             hand_head(me.core, h).wait_send()
 
     plan = {
-        (0, 0): [lambda: kv_stage(1, 1)],
-        (0, 2): [lambda: late_arrival(2), lambda: kv_stage(1, 2)],
+        (0, 0): [lambda: kv_stage(1, 1), lambda: late_arrival(2)],
+        (0, 1): [lambda: late_projection(2)],
+        (0, 2): [lambda: kv_stage(1, 2), lambda: kv_stage(2, 1), lambda: late_arrival(3)],
         (0, 3): [lambda: rs_stage(0, 0)],
-        (0, 4): [lambda: late_projection(2)],
-        (1, 1): [lambda: kv_stage(2, 1), lambda: rs_stage(0, 1)],
-        (1, 2): [lambda: late_arrival(3), lambda: rs_stage(0, 2), lambda: kv_stage(2, 2)],
+        (0, 4): [lambda: late_projection(3), lambda: kv_stage(1, 3)],
+        (1, 1): [lambda: kv_stage(2, 2), lambda: rs_stage(0, 1)],
+        (1, 2): [lambda: kv_stage(3, 1), lambda: rs_stage(0, 2)],
         (1, 3): [lambda: rs_stage(1, 0)],
-        (1, 4): [lambda: late_projection(3), weights_left, lambda: weight_terms(0)],
-        (2, 0): [lambda: kv_stage(3, 1)],
-        (2, 1): [lambda: rs_stage(1, 1), lambda: xr_begin(0)],
-        (2, 2): [lambda: kv_stage(3, 2), lambda: rs_stage(1, 2)],
+        (1, 4): [weights_left, lambda: kv_stage(2, 3), lambda: kv_stage(3, 2)],
+        (2, 1): [lambda: rs_stage(0, 3), lambda: weight_terms(0), lambda: rs_stage(1, 1)],
+        (2, 2): [lambda: xr_begin(0), lambda: rs_stage(1, 2)],
         (2, 3): [lambda: rs_stage(2, 0)],
-        (2, 4): [lambda: weight_terms(1)],
-        (3, 1): [lambda: rs_stage(2, 1), lambda: xr_end(0), lambda: xr_begin(1)],
-        (3, 2): [lambda: rs_stage(2, 2), lambda: ws_stage(0, 1)],
-        (3, 3): [lambda: rs_stage(3, 0)],
-        (3, 4): [lambda: weight_terms(2), lambda: ws_stage(0, 2), lambda: xr_end(1)],
+        (2, 4): [lambda: rs_stage(1, 3), lambda: weight_terms(1), lambda: kv_stage(3, 3)],
+        (3, 1): [lambda: rs_stage(2, 1), lambda: xr_begin(1)],
+        (3, 2): [lambda: rs_stage(2, 2), lambda: xr_end(0)],
+        (3, 3): [lambda: rs_stage(3, 0), lambda: ws_stage(0, 1)],
+        (3, 4): [lambda: rs_stage(2, 3), lambda: weight_terms(2)],
     }
 
     def one_head(h, carry):
@@ -720,7 +770,6 @@
                     for item in plan[head, point]:
                         item()
 
-        load_head(h)
         serve(0)
         attend(h, 0)
         serve(1)
@@ -729,6 +778,11 @@
         key_terms(h)
         serve(3)
         store_head(h)
+
+        @pl.when(h < HEADS - 1)
+        def _():
+            load_head(h + 1)
+
         serve(4)
         return carry
 
@@ -770,25 +824,31 @@
     early_heads, late_head = pl.ds(0, HEADS - 1), pl.ds(HEADS - 1, 1)
     rs_stage(3, 1)
     xr_begin(2)
-    ws_stage(1, 1)
+    ws_stage(0, 2)
     rs_stage(3, 2)
+    xr_end(1)
+    ws_stage(0, 3)
+    rs_stage(3, 3)
     mean = weight_terms(3) * (1.0 / FEATURES)
     pair_sum(3)
     ws_stage(3, 0)
-    ws_stage(1, 2)
-    xr_end(2)
-
-    def row_grad(r, carry):
-        dx = inv_ref[...] * (ngrad[:, columns_of(r)] - unit_piece(r) * mean)
-        x_ref[:, columns_of(r)] = dx.astype(BF16)
+    ws_stage(1, 1)
+
+    def row_grad(j, carry):
+        dx = inv_ref[...] * (ngrad[j] - unit_piece(j) * mean)
+        x_ref[:, columns_of(j)] = dx.astype(BF16)
         return carry
 
-    lax.fori_loop(0, RANKS, row_grad, 0)
+    lax.fori_loop(0, 4, row_grad, 0)
     stores.append(pltpu.make_async_copy(x_ref, dx_hbm, io_sem.at[2]))
     stores[2].start()
     ws_stage(3, 1)
+    ws_stage(1, 2)
+    xr_end(2)
+    ws_stage(3, 2)
+    ws_stage(1, 3)
     ws_stage(2, 1)
-    ws_stage(3, 2)
+    ws_stage(3, 3)
     xr_stage(3, 0)
     gains = [
         x_copy(5 + d, x_send.at[pl.ds(PART, 16)], x_gain.at[d - 1], me.along_x(d))
@@ -797,10 +857,11 @@
     for copy in gains:
         copy.start()
     ws_stage(2, 2)
-    spread_start(0, early_heads)
     xr_stage(3, 1)
     final[me.core, HEADS - 1, piece_rows(me.x)] = x_send[piece_rows(me.x), :]
     spread_start(3, late_head)
+    ws_stage(2, 3)
+    spread_start(0, early_heads)
     spread_wait(0, early_heads)
     to_partner(9, early_heads, me.core).start()
     for copy in gains:
@@ -844,33 +905,19 @@
 
 
 def settle(*refs):
-    count = len(refs) // 2
-    for n in range(count):
-        refs[count + n][...] = refs[n][...]
+    for n in range(5):
+        refs[6 + n][...] = refs[n][...]
+    refs[11][...] = refs[5][0, :]
 
 
 def local(inputs, queries, out_grad, span_ids, norm_gain, key_weight, value_weight):
-    rank = lax.axis_index("shard") * 8 + lax.axis_index("ctx")
-    spans = span_ids.reshape(RANKS, 2)
-    own = lax.dynamic_slice_in_dim(spans, rank, 1, 0).reshape(2, 1)
-    token = jnp.arange(SPAN, dtype=jnp.int32)[None, :]
-    own_pos = (own * SPAN + token).reshape(ROWS)
-    ordered = spans.reshape(2, 2, 4, 2).transpose(1, 0, 2, 3).reshape(RANKS, 2)
-    low = jnp.minimum(ordered[:, 0], ordered[:, 1])[:, None] * SPAN + token
-    high = jnp.maximum(ordered[:, 0], ordered[:, 1])[:, None] * SPAN + token
-    kpos = jnp.stack([low.reshape(-1), high.reshape(-1)])
-    half = HEAD // 2
-    frequency = jnp.exp(
-        -math.log(ROPE_BASE) * (2.0 * jnp.arange(half, dtype=jnp.float32) / HEAD)
-    )
-    angles = own_pos.astype(jnp.float32)[:, None] * frequency[None, :]
-    cosine, sine = jnp.cos(angles), jnp.sin(angles)
-    cosine = jnp.concatenate([cosine, cosine], axis=1)
-    sine = jnp.concatenate([-sine, sine], axis=1)
-
+    frequency = np.exp(
+        -math.log(ROPE_BASE) * (2.0 * np.arange(HEAD // 2, dtype=np.float32) / HEAD)
+    ).astype(np.float32)
+    frequency = jnp.asarray(np.concatenate([frequency, frequency])[None, :])
+    anywhere = pl.BlockSpec(memory_space=pl.ANY)
     vmem = pl.BlockSpec(memory_space=pltpu.VMEM)
     smem = pl.BlockSpec(memory_space=pltpu.SMEM)
-    anywhere = pl.BlockSpec(memory_space=pl.ANY)
     dma = pltpu.SemaphoreType.DMA
     outs = pl.pallas_call(
         kernel,
@@ -882,7 +929,7 @@
             jax.ShapeDtypeStruct((SHARE, WIDTH), F32),
             jax.ShapeDtypeStruct((8, SHARE), F32),
         ],
-        in_specs=[anywhere] * 3 + [smem] + [vmem] * 6,
+        in_specs=[anywhere] * 3 + [smem, vmem] + [anywhere] * 2 + [vmem],
         out_specs=[anywhere] * 3 + [vmem] * 3,
         scratch_shapes=[
             pltpu.VMEM((ROWS, FEATURES), BF16),
@@ -900,17 +947,22 @@
             pltpu.VMEM((2 * WIDTH, RANKS * SPAN), BF16),
             pltpu.VMEM((WIDTH, RANKS * SPAN), BF16),
             pltpu.VMEM((HEADS, 2, 4, 4, 2, SPAN, HEAD), BF16),
-            pltpu.VMEM((HEADS, 2, 3, 4, 2, SPAN, HEAD), BF16),
+            pltpu.VMEM((HEADS, 2, 2, 4, SPAN, HEAD), BF16),
+            pltpu.VMEM((HEADS, 2, 2, 4, 2, SPAN, HEAD), BF16),
             pltpu.VMEM((HEADS, 2, 3, 2, SPAN, HEAD), BF16),
             pltpu.VMEM((HEADS, ROWS, 2 * HEAD), BF16),
-            pltpu.VMEM((ROWS, FEATURES), F32),
-            pltpu.VMEM((RANKS, SHARE, ROWS), BF16),
+            pltpu.VMEM((4, ROWS, FOUR), F32),
+            pltpu.VMEM((4, ROWS, FOUR), BF16),
+            pltpu.VMEM((4, FOUR, ROWS), BF16),
+            pltpu.VMEM((4, 1, FOUR), F32),
             pltpu.VMEM((4, 4, 2, BLOCK, 2 * HEAD), BF16),
             pltpu.VMEM((4, 4, BLOCK, 2 * HEAD), BF16),
             pltpu.VMEM((HEADS - 1, 4, 4, PART, 2 * HEAD), BF16),
-            pltpu.VMEM((HEADS - 1, 2, 3, 4, 32, HEAD), BF16),
+            pltpu.VMEM((HEADS - 1, 2, 2, 4, 16, HEAD), BF16),
+            pltpu.VMEM((HEADS - 1, 2, 2, 4, 32, HEAD), BF16),
             pltpu.VMEM((HEADS - 1, 2, 3, 32, HEAD), BF16),
-            pltpu.VMEM((2, 3, 4, 80, 2 * HEAD), BF16),
+            pltpu.VMEM((2, 2, 4, 48, 2 * HEAD), BF16),
+            pltpu.VMEM((2, 2, 4, 80, 2 * HEAD), BF16),
             pltpu.VMEM((2, 3, 80, 2 * HEAD), BF16),
             pltpu.VMEM((HEADS - 1, 3, 4, 4, 32, 2 * HEAD), BF16),
             pltpu.VMEM((3, 32, 2 * HEAD), BF16),
@@ -918,14 +970,17 @@
             pltpu.VMEM((3, 16, 2 * HEAD), BF16),
             pltpu.VMEM((2, HEADS, PART, 2 * HEAD), BF16),
             pltpu.VMEM((ROWS, 1), F32),
-            dma((3,)),
-            dma((EARLY + 1, 2, 6)), dma((EARLY + 1, 2, 6)),
+            pltpu.VMEM((2, RANKS * SPAN), jnp.int32),
+            pltpu.VMEM((ROWS, HEAD), F32),
+            pltpu.VMEM((ROWS, HEAD), F32),
+            dma((3 + 2 * HEADS,)),
+            dma((EARLY + 1, 2, 7)), dma((EARLY + 1, 2, 7)),
             dma((7 + HEADS,)), dma((7 + HEADS,)),
             dma((HEADS - EARLY, 3)), dma((HEADS - EARLY, 3)),
-            dma((HEADS, 2, 6)), dma((HEADS, 2, 6)),
-            dma((HEADS, 2, 6)), dma((HEADS, 2, 6)),
+            dma((HEADS, 2, 7)), dma((HEADS, 2, 7)),
+            dma((HEADS, 2, 7)), dma((HEADS, 2, 7)),
             dma((HEADS, 4)), dma((HEADS, 4)),
-            dma((HEADS, 2, 6)), dma((HEADS, 2, 6)),
+            dma((HEADS, 2, 7)), dma((HEADS, 2, 7)),
             dma((HEADS, 3)), dma((HEADS, 3)),
             dma((11,)), dma((11,)),
         ],
@@ -937,21 +992,21 @@
         ),
         name="layer",
     )(
-        inputs, queries, out_grad, spans.reshape(-1), kpos, norm_gain.reshape(1, SHARE),
-        key_weight, value_weight, cosine, sine,
+        inputs, queries, out_grad, span_ids, norm_gain, key_weight, value_weight, frequency
     )
     blocks = [pl.BlockSpec((ROWS, FEATURES // 4), lambda i: (0, i))] * 3
     blocks += [pl.BlockSpec((SHARE // 4, WIDTH), lambda i: (i, 0))] * 2
-    blocks += [pl.BlockSpec((8, SHARE), lambda i: (0, 0))]
+    gains = [pl.BlockSpec((8, SHARE), lambda i: (0, 0)), pl.BlockSpec((SHARE,), lambda i: (0,))]
     outs = pl.pallas_call(
         settle,
-        out_shape=[jax.ShapeDtypeStruct(o.shape, o.dtype) for o in outs],
+        out_shape=[jax.ShapeDtypeStruct(o.shape, o.dtype) for o in outs[:5]]
+        + [jax.ShapeDtypeStruct((SHARE,), F32)],
         grid=(4,),
-        in_specs=blocks,
-        out_specs=blocks,
+        in_specs=blocks + gains[:1],
+        out_specs=blocks + gains[1:],
         name="settle",
     )(*outs)
-    return (*outs[:5], outs[5][0])
+    return tuple(outs)
 
 
 def solution(mesh):

time: 167 us -> 153 us (0.916)
  Pallas kernels: 159 us -> 151 us
  local copies, waits for them, and re-layouts: 4.24 us -> 1.35 us
  other arithmetic: 2.02 us -> 0 us
    pallas_call x1, Pallas kernels: 155 us -> 146 us  [local(): pl.pallas_call(kernel, out_shape=[jax.ShapeDtypeStruct((ROWS, FEATURES),...]
where the time goes in v3:
time: 153 us
  Pallas kernels  151 us (99%)
    pallas_call x1, Pallas kernels, local(): pl.pallas_call(kernel, out_shape=[jax.ShapeDtypeStruct((ROWS, FEATURES),...  146 us
    pallas_call x1, Pallas kernels, local(): pl.pallas_call(settle, out_shape=[jax.ShapeDtypeStruct(o.shape, o.dtype)...  4.79 us

profile of v3, /device:TPU:1, one launch (start us, length us, event | category | flops | bytes accessed | tf_op | source)
XLA Modules:
  0.0 153.2 jit_solution(15912960220646329094)
XLA Ops:
  0.6 1.4 copy.14.spans_ref
  2.0 146.2 %layer.1 = (bf16[128,4096]{1,0:T(8,128)(2,1)}, bf16[128,4096]{1,0:T(8,128)(2,1)}, bf16[128,4096]{1,0:T(8,128)(2,1)}, f32[256,512]{1,0:T(8,128)}, f32[256,512]{1,0:T(8,128)}, /*index=5*/f32[8,256]{1,0:T(8,128)}) custom-call(bf16[128,4096]{1,0:T(8,128)(2,1)} %x_hbm.1, bf16[128,4096]{1,0:T(8,128)(2,1)} %q_hbm.1, bf16[128,4096]{1,0:T(8,128)(2,1)} %g_hbm.1, ...), custom_call_target="tpu_custom_call" | custom-call | flops 12000000000 | bytes 10000000 | tf_op jit(solution)/shard_map/layer/pallas_call | solution.py:922
  148.2 4.8 %settle.1 = (bf16[128,4096]{1,0:T(8,128)(2,1)}, bf16[128,4096]{1,0:T(8,128)(2,1)}, bf16[128,4096]{1,0:T(8,128)(2,1)}, f32[256,512]{1,0:T(8,128)}, f32[256,512]{1,0:T(8,128)}, /*index=5*/f32[256]{0:T(256)}) custom-call(bf16[128,4096]{1,0:T(8,128)(2,1)} %get-tuple-element.12.refs_0_, bf16[128,4096]{1,0:T(8,128)(2,1)} %get-tuple-element.13.refs_1_, ...), custom_call_target="tpu_custom_call" | custom-call | tf_op jit(solution)/shard_map/settle/pallas_call | solution.py:1000

commit v4 on v3

--- a/solution.py
+++ b/solution.py
@@ -83,6 +83,8 @@
 
 
 class Route:
+    direct = False
+
     def __init__(self, place, kind, slot, half, send, recv):
         self.place, self.kind, self.slot, self.half = place, kind, slot, half
         self.send_sems, self.recv_sems = send, recv
@@ -112,15 +114,21 @@
         )
 
     def drain(self):
-        for n in range(7):
+        for n in self.direct_copies if self.direct else range(7):
             self.message(n).wait_send()
 
 
 class Gather(Route):
+    direct_copies = range(6)
+
     def message(self, n, back=False):
         if n < 3:
             ref = self.block(4 - STEPS[n] if back else 0, 0)
             return self.copy(n, ref, ref, self.device(STEPS[n], 0))
+        if self.direct:
+            step = STEPS[n - 3]
+            ref = self.column(4 - step if back else 0)
+            return self.copy(n, ref, ref, self.device(0, step))
         step = 1 if n % 2 else 3
         if n < 5:
             ref = self.column(4 - step if back else 0)
@@ -134,8 +142,12 @@
         elif number == 1:
             for n in range(3):
                 self.message(n, True).wait_recv()
-            start_all([self.message(n) for n in (3, 4)])
+            start_all([self.message(n) for n in ((3, 4, 5) if self.direct else (3, 4))])
             arrived(0)
+        elif self.direct:
+            for n in (3, 4, 5) if number == 2 else ():
+                self.message(n, True).wait_recv()
+                arrived(4 - STEPS[n - 3])
         elif number == 2:
             for n, db in ((3, 3), (4, 1)):
                 self.message(n, True).wait_recv()
@@ -148,11 +160,16 @@
 
 
 class Scatter(Route):
+    direct_copies = (0, 1, 2, 4, 5, 6)
+
     def __init__(self, place, kind, slot, half, halves, columns, blocks, send, recv):
         super().__init__(place, kind, slot, half, send, recv)
         self.halves, self.columns, self.blocks = halves, columns, blocks
 
     def message(self, n):
+        if n < 3 and self.direct:
+            step = STEPS[n]
+            return self.copy(n, self.column(step), self.columns(n), self.device(0, step))
         if n < 4:
             step = 3 if n % 2 else 1
             if n < 2:
@@ -165,18 +182,21 @@
 
     def stage(self, number):
         if number == 0:
-            start_all([self.message(n) for n in range(2)])
+            start_all([self.message(n) for n in range(3 if self.direct else 2)])
         elif number == 1:
-            for n, step in ((0, 1), (1, 3)):
+            for n, step in () if self.direct else ((0, 1), (1, 3)):
                 self.message(n).wait_recv()
                 add_into(self.half(self.column(step), n), [self.halves(n)])
                 self.message(n + 2).start()
         elif number == 2:
-            for n in (2, 3):
+            for n in (0, 1, 2) if self.direct else (2, 3):
                 self.message(n).wait_recv()
             for n, step in enumerate(STEPS + (0,)):
                 place = (self.a + step) % 4
-                add_into(self.block(step, 0), [self.columns(i).at[place] for i in range(2)])
+                add_into(
+                    self.block(step, 0),
+                    [self.columns(i).at[place] for i in range(3 if self.direct else 2)],
+                )
                 if step:
                     self.message(4 + n).start()
         else:
@@ -247,8 +267,8 @@
     x_hbm, q_hbm, g_hbm, spans_ref, gain_ref, wk_hbm, wv_hbm, frequency_ref,
     out_hbm, dq_hbm, dx_hbm, dwk_ref, dwv_ref, dgain_ref,
     x_ref, q_ref, g_ref, w_first, w_rest, kvbuf, qs, gs, qt, gt, probs_low, probs_high, ds_low, ds_high,
-    grads, kv_halves, kv_columns, kv_blocks, dkv, ngrad, normed, normed_t, gain_row, t_last, p_last, p_rest, q_halves, q_columns, q_blocks,
-    w_halves, w_columns, w_blocks, r_land, l_land, x_send, x_gain, final, inv_ref, kpos_ref, cos_ref, sin_ref,
+    grads, kv_halves, kv_columns, kv_third, kv_blocks, dkv, ngrad, normed, normed_t, gain_row, t_last, p_last, p_rest, q_halves, q_columns, q_blocks,
+    w_halves, w_columns, w_third, w_blocks, r_land, l_land, x_send, x_gain, final, inv_ref, kpos_ref, cos_ref, sin_ref,
     io_sem, w_send, w_recv, hand_send, hand_recv, wx_send, wx_recv, kv_send, kv_recv,
     rs_send, rs_recv, pair_send, pair_recv, ws_send, ws_recv, xr_send, xr_recv, x_ssem, x_rsem,
 ):
@@ -400,7 +420,9 @@
                 lambda z, y, h=h, kind=kind: grads.at[h, kind, z, y],
                 lambda ref, n: ref.at[:, n],
                 lambda n, h=h, kind=kind: kv_halves.at[h, kind, n],
-                lambda n, h=h, kind=kind: kv_columns.at[h, kind, n],
+                lambda n, h=h, kind=kind: (
+                    kv_columns.at[h, kind, n] if n < 2 else kv_third.at[kind]
+                ),
                 lambda n, h=h, kind=kind: kv_blocks.at[h, kind, n],
                 rs_send.at[h, kind],
                 rs_recv.at[h, kind],
@@ -500,7 +522,9 @@
                 lambda z, y, kind=kind: t_last.at[z, y, me.core, tall_rows(kind, True)],
                 lambda ref, n, kind=kind: tall_half(ref, kind, True, n),
                 lambda n, kind=kind: w_halves.at[kind, n, :, pl.ds(0, 48 if kind and n else 32)],
-                lambda n, kind=kind: w_columns.at[kind, n, :, pl.ds(0, 80 if kind else 64)],
+                lambda n, kind=kind: (w_columns.at[kind, n] if n < 2 else w_third.at[kind]).at[
+                    :, pl.ds(0, 80 if kind else 64)
+                ],
                 lambda n, kind=kind: w_blocks.at[kind, n, pl.ds(0, 80 if kind else 64)],
                 ws_send.at[HEADS - 1, kind],
                 ws_recv.at[HEADS - 1, kind],
@@ -690,6 +714,9 @@
         project(h)
         kv_stage(h, 0)
 
+    for routes in (w_routes[0], late_routes, kv_routes[0], rs_routes[3], ws_routes[3]):
+        for route in routes:
+            route.direct = True
     late_stage(0)
     w_stage(0, 0)
     positions()
@@ -698,11 +725,9 @@
     late_stage(1)
     w_stage(0, 1)
     late_stage(2)
-    w_stage(0, 2)
-    late_stage(3)
     for h in range(EARLY, HEADS):
         wx[h].stage(0)
-    w_stage(0, 3)
+    w_stage(0, 2)
     for kind in range(2):
         for db in range(4):
             hand_column(1 - me.core, kind, db).wait_recv()
@@ -712,12 +737,11 @@
     turn()
     kv_stage(0, 1)
     late_arrival(1)
-    kv_stage(0, 2)
-    late_projection(1)
     loads[1].wait()
     loads[2].wait()
     load_head(0)
-    kv_stage(0, 3)
+    late_projection(1)
+    kv_stage(0, 2)
 
     def xr_begin(h):
         pair_sum(h)
@@ -822,7 +846,6 @@
             spread(base, heads, d, (me.x + 4 - d) % 4).wait_recv()
 
     early_heads, late_head = pl.ds(0, HEADS - 1), pl.ds(HEADS - 1, 1)
-    rs_stage(3, 1)
     xr_begin(2)
     ws_stage(0, 2)
     rs_stage(3, 2)
@@ -842,7 +865,6 @@
     lax.fori_loop(0, 4, row_grad, 0)
     stores.append(pltpu.make_async_copy(x_ref, dx_hbm, io_sem.at[2]))
     stores[2].start()
-    ws_stage(3, 1)
     ws_stage(1, 2)
     xr_end(2)
     ws_stage(3, 2)
@@ -949,6 +971,7 @@
             pltpu.VMEM((HEADS, 2, 4, 4, 2, SPAN, HEAD), BF16),
             pltpu.VMEM((HEADS, 2, 2, 4, SPAN, HEAD), BF16),
             pltpu.VMEM((HEADS, 2, 2, 4, 2, SPAN, HEAD), BF16),
+            pltpu.VMEM((2, 4, 2, SPAN, HEAD), BF16),
             pltpu.VMEM((HEADS, 2, 3, 2, SPAN, HEAD), BF16),
             pltpu.VMEM((HEADS, ROWS, 2 * HEAD), BF16),
             pltpu.VMEM((4, ROWS, FOUR), F32),
@@ -963,6 +986,7 @@
             pltpu.VMEM((HEADS - 1, 2, 3, 32, HEAD), BF16),
             pltpu.VMEM((2, 2, 4, 48, 2 * HEAD), BF16),
             pltpu.VMEM((2, 2, 4, 80, 2 * HEAD), BF16),
+            pltpu.VMEM((2, 4, 80, 2 * HEAD), BF16),
             pltpu.VMEM((2, 3, 80, 2 * HEAD), BF16),
             pltpu.VMEM((HEADS - 1, 3, 4, 4, 32, 2 * HEAD), BF16),
             pltpu.VMEM((3, 32, 2 * HEAD), BF16),

time: 153 us -> 150 us (0.980)
  Pallas kernels: 151 us -> 148 us
    pallas_call x1, Pallas kernels: 146 us -> 143 us  [local(): pl.pallas_call(kernel, out_shape=[jax.ShapeDtypeStruct((ROWS, FEATURES),...]
where the time goes in v4:
time: 150 us
  Pallas kernels  148 us (99%)
    pallas_call x1, Pallas kernels, local(): pl.pallas_call(kernel, out_shape=[jax.ShapeDtypeStruct((ROWS, FEATURES),...  143 us
    pallas_call x1, Pallas kernels, local(): pl.pallas_call(settle, out_shape=[jax.ShapeDtypeStruct(o.shape, o.dtype)...  4.79 us

profile of v4, /device:TPU:1, one launch (start us, length us, event | category | flops | bytes accessed | tf_op | source)
XLA Modules:
  0.0 149.7 jit_solution(16896859581467598857)
XLA Ops:
  0.6 1.4 copy.14.spans_ref
  2.0 142.8 %layer.1 = (bf16[128,4096]{1,0:T(8,128)(2,1)}, bf16[128,4096]{1,0:T(8,128)(2,1)}, bf16[128,4096]{1,0:T(8,128)(2,1)}, f32[256,512]{1,0:T(8,128)}, f32[256,512]{1,0:T(8,128)}, /*index=5*/f32[8,256]{1,0:T(8,128)}) custom-call(bf16[128,4096]{1,0:T(8,128)(2,1)} %x_hbm.1, bf16[128,4096]{1,0:T(8,128)(2,1)} %q_hbm.1, bf16[128,4096]{1,0:T(8,128)(2,1)} %g_hbm.1, ...), custom_call_target="tpu_custom_call" | custom-call | flops 12000000000 | bytes 10000000 | tf_op jit(solution)/shard_map/layer/pallas_call | solution.py:944
  144.7 4.8 %settle.1 = (bf16[128,4096]{1,0:T(8,128)(2,1)}, bf16[128,4096]{1,0:T(8,128)(2,1)}, bf16[128,4096]{1,0:T(8,128)(2,1)}, f32[256,512]{1,0:T(8,128)}, f32[256,512]{1,0:T(8,128)}, /*index=5*/f32[256]{0:T(256)}) custom-call(bf16[128,4096]{1,0:T(8,128)(2,1)} %get-tuple-element.12.refs_0_, bf16[128,4096]{1,0:T(8,128)(2,1)} %get-tuple-element.13.refs_1_, ...), custom_call_target="tpu_custom_call" | custom-call | tf_op jit(solution)/shard_map/settle/pallas_call | solution.py:1024
